TPU v7x, 32 devices: a whole 2x2x4 slice. The times are simulated.
32 devices in a mesh: dom: 8 (over z, x), feat: 4 (over y, core).
Axes of the slice: x: 2, y: 2, z: 4, core: 2. Of those that a mesh axis runs over, the one named last changes fastest.
Arguments:
- embed: bfloat16 [256, 8192], P('feat', 'dom'), may hold values from -6 to 6
- weight: bfloat16 [256, 256], P('feat'), may hold values from -0.375 to 0.375
- cotangent: bfloat16 [256, 8192], P('feat', 'dom'), may hold values from -6 to 6
- edge_masks: int32 [768, 128, 128], P('dom'), may hold values 0 or 1
- tile_rows: int32 [768], P('dom'), may hold values from 0 to 7
- tile_owner: int32 [768, 1], P('dom'), may hold values from 0 to 7; in each aligned block of 96 rows (0 to 95, 96 to 191, ...) at most 24 rows name the same one
- tile_sub: int32 [768], P('dom'), may hold values from 0 to 7
Outputs:
- output: bfloat16 [256, 8192], P('feat', 'dom')
- embed_grad: float32 [256, 8192], P('feat', 'dom')
- weight_grad: float32 [256, 256], P('feat')
Inputs may be any that keep to these rules, and one draw needn't show every extreme that they name: `tile_owner`: among the 96 tiles of one index of dom no owner is named more than 24 times, a bound that some block reaches.
All inputs are finite; a program needn't handle non-finite values. No bound on the sum of `edge_masks` on one device may be relied on, other than what follows from the above.
Results may differ from a plain program's by a relative error of at most 0.0059.
Values may be sent and summed in bfloat16 or wider, within the bound.
A program may use at most 64 MiB of HBM per device.

v0:
```python
import math

import jax
import jax.numpy as jnp
from jax import lax
from jax.sharding import PartitionSpec as P


def per_device(embed, weight, cotangent, edge_masks, tile_rows, tile_owner, tile_sub):
    feat_width = embed.shape[0]
    local_nodes = embed.shape[1]
    block_len = edge_masks.shape[1]
    local_blocks = local_nodes // block_len
    dom_count = lax.axis_size("dom")
    nodes_all = local_nodes * dom_count
    block_range = jnp.arange(local_blocks, dtype=jnp.int32)
    col_ids = tile_owner[:, 0] * local_blocks + tile_sub
    own_bf = embed.reshape(feat_width, local_blocks, block_len)
    gathered = lax.all_gather(embed, "dom", axis=1, tiled=True)
    all_blocks = gathered.reshape(feat_width, dom_count * local_blocks, block_len)
    fetched = jnp.take(all_blocks, col_ids, axis=1)
    mask_bf = edge_masks.astype(jnp.bfloat16)
    contrib = jnp.einsum("ftj,tij->fti", fetched, mask_bf, preferred_element_type=jnp.float32)
    row_onehot = (tile_rows[:, None] == block_range[None, :]).astype(jnp.float32)
    neighbour = jnp.einsum("fti,tr->fri", contrib, row_onehot, precision=lax.Precision.HIGHEST)
    row_int = (tile_rows[:, None] == block_range[None, :]).astype(jnp.int32)
    counts = jnp.sum(edge_masks, axis=2)
    degree = jnp.dot(row_int.T, counts)
    inv_root = 1.0 / jnp.sqrt(1.0 + degree.astype(jnp.float32))
    own_blocks = own_bf.astype(jnp.float32)
    aggregate = (
        (own_blocks + neighbour * inv_root[None])
        .astype(jnp.bfloat16)
        .reshape(feat_width, local_nodes)
    )
    pre_act = lax.psum_scatter(
        jnp.einsum("fh,fn->hn", weight, aggregate, preferred_element_type=jnp.float32),
        "feat",
        scatter_dimension=0,
        tiled=True,
    )
    gate_vals = jax.nn.sigmoid(pre_act)
    output = (pre_act * gate_vals).astype(jnp.bfloat16)
    grad_pre = (
        cotangent.astype(jnp.float32) * gate_vals * (1.0 + pre_act * (1.0 - gate_vals))
    ).astype(jnp.bfloat16)
    grad_full = lax.all_gather(grad_pre, "feat", axis=0, tiled=True)
    grad_agg = jnp.einsum("fh,hn->fn", weight, grad_full, preferred_element_type=jnp.float32)
    weight_terms = jnp.einsum("fn,hn->fh", aggregate, grad_full, preferred_element_type=jnp.float32)
    grad_blocks = grad_agg.reshape(feat_width, local_blocks, block_len)
    scaled_grad = (grad_blocks * inv_root[None]).astype(jnp.bfloat16)
    selected = jnp.take(scaled_grad, tile_rows, axis=1)
    partials = jnp.einsum("fti,tij->tfj", selected, mask_bf, preferred_element_type=jnp.float32)
    start = jnp.int32(0)
    inside = (col_ids >= start) & (col_ids < start + lax.axis_size("dom") * local_blocks)
    target = jnp.where(inside, col_ids, lax.axis_size("dom") * local_blocks)
    empty = jnp.zeros((lax.axis_size("dom") * local_blocks, feat_width, block_len), jnp.float32)
    received = lax.psum_scatter(
        empty.at[target].add(partials, mode="drop"), "dom", scatter_dimension=0, tiled=True
    )
    incoming = jnp.transpose(received, (1, 0, 2))
    embed_grad = (grad_blocks + incoming).reshape(feat_width, local_nodes)
    weight_grad = lax.psum(weight_terms, "dom") / math.sqrt(nodes_all)
    return (output, embed_grad, weight_grad)


def solution(mesh):
    in_specs = (
        P("feat", "dom"),
        P("feat", None),
        P("feat", "dom"),
        P("dom", None, None),
        P("dom"),
        P("dom", None),
        P("dom"),
    )
    out_specs = (P("feat", "dom"), P("feat", "dom"), P("feat", None))
    return jax.shard_map(
        per_device, mesh=mesh, in_specs=in_specs, out_specs=out_specs, check_vma=False
    )
```

profile of v0, /device:TPU:0, one launch (start us, length us, event | category | flops | bytes accessed | tf_op | source)
XLA Modules:
  0.0 247.1 jit_solution(7143764751583575649)
XLA Ops:
  7.2 0.7 all-gather.2.cloned.1.call-update
  8.0 0.9 convert_bitcast_fusion
  9.0 4.5 %reduce_sum.9 = s32[96,128]{1,0:T(8,128)S(1)} reduce(s32[96,128,128]{2,1,0:T(8,128)} %param.10, s32[]{:T(128)} %constant.14.clone.1), dimensions={2}, to_apply=%region_0.1 | reduce | flops 1560576 | bytes 6340612 | tf_op jit(solution)/shard_map/reduce_sum | solution.py:27
  13.7 39.4 %all-gather.2.cloned.1.call-done = bf16[64,8192]{1,0:T(8,128)(2,1)} async-done(((bf16[64,1024]{1,0:T(8,128)(2,1)}), bf16[64,8192]{1,0:T(8,128)(2,1)}) %all-gather.2.cloned.1.call-update) | async-done | bytes 1048592 | tf_op jit(solution)/shard_map/all_gather | solution.py:19
  53.1 1.5 copy_bitcast_fusion
  54.6 0.9 gather_fusion
  55.5 5.0 %convolution_bitcast_fusion = f32[64,96,128]{2,0,1:T(8,128)S(1)} fusion(bf16[96,64,128]{2,1,0:T(8,128)(2,1)S(1)} %gather_fusion, s32[96,128,128]{2,1,0:T(8,128)} %param.10, pred[96]{0:T(512)(128)(4,1)S(1)} %get-tuple-element.15), kind=kOutput, calls=%fused_computation.5 | convolution fusion | flops 203685888 | bytes 11010144 | tf_op jit(solution)/shard_map/ftj,tij->fti/dot_general | solution.py:23
  60.5 2.9 %fusion.20 = bf16[64,8,128]{2,1,0:T(8,128)(2,1)S(1)} fusion(f32[64,8,128]{2,1,0:T(8,128)S(1)} %bitcast.67, f32[64,96,128]{2,0,1:T(8,128)S(1)} %convolution_bitcast_fusion, f32[8,128]{1,0:T(8,128)S(1)} %fusion.24, s32[96]{0:T(128)S(1)} %copy-done.3), kind=kOutput, calls=%fused_computation.20 | convolution fusion | flops 75694848 | bytes 3543424 | tf_op jit(solution)/shard_map/fti,tr->fri/dot_general | solution.py:25
  63.4 0.3 convolution_bitcast_fusion.1
  63.8 1.3 copy.39
  65.2 23.7 %reduce-scatter.7.cloned.1.call-done = f32[64,1024]{1,0:T(8,128)} async-done(((f32[256,1024]{1,0:T(8,128)}), f32[64,1024]{1,0:T(8,128)}) %reduce-scatter.7.cloned.1.call-update) | async-done | bytes 262160 | tf_op jit(solution)/shard_map/reduce_scatter | solution.py:36
  88.9 1.7 multiply_convert_fusion
  90.6 6.8 %all_gather.7 = bf16[256,1024]{1,0:T(8,128)(2,1)S(1)} all-gather(bf16[64,1024]{1,0:T(8,128)(2,1)S(1)} %get-tuple-element.17), channel_id=1, replica_groups=mesh['dom'=8,'feat'=4] {'feat'}, dimensions={0}, use_global_device_ids=true | all-gather | bytes 655360 | tf_op jit(solution)/shard_map/all_gather | solution.py:47
  97.4 0.9 fusion.29
  98.3 0.2 convolution_bitcast_fusion.2
  98.6 0.8 gather_fusion.1
  99.5 5.5 %fusion.2 = f32[96,64,128]{2,1,0:T(8,128)} fusion(bf16[96,64,128]{2,1,0:T(8,128)(2,1)S(1)} %gather_fusion.1, s32[96,128,128]{2,1,0:T(8,128)} %param.10, pred[96]{0:T(512)(128)(4,1)S(1)} %compare_and_fusion), kind=kOutput, calls=%fused_computation.6 | convolution fusion | flops 203685888 | bytes 11010144 | tf_op jit(solution)/shard_map/fti,tij->tfj/dot_general | solution.py:53
  104.9 0.2 broadcast_in_dim.39
  105.2 10.2 %scatter_fusion = f32[64,64,128]{2,1,0:T(8,128)S(1)} fusion(f32[64,64,128]{2,1,0:T(8,128)S(1)} %broadcast_in_dim.39, s32[96]{0:T(128)S(1)} %compare_select_fusion.1, f32[96,64,128]{2,1,0:T(8,128)} %fusion.2), kind=kCustom, calls=%fused_computation.2 | custom fusion | flops 786432 | bytes 9437568 | tf_op jit(solution)/shard_map/scatter-add | solution.py:59
  115.4 1.3 copy-done.1
  116.8 50.7 %all-reduce.2.cloned.1.call-done = f32[64,256]{1,0:T(8,128)} async-done(((f32[64,256]{1,0:T(8,128)}), f32[64,256]{1,0:T(8,128)}) %all-reduce.2.cloned.1.call-update) | async-done | bytes 65552 | tf_op jit(solution)/shard_map/psum | solution.py:63
  167.5 1.5 broadcast_multiply_fusion
  169.0 69.9 %reduce-scatter.5.cloned.1.call-done = f32[8,64,128]{2,1,0:T(8,128)} async-done(((f32[64,64,128]{2,1,0:T(8,128)}), f32[8,64,128]{2,1,0:T(8,128)}) %reduce-scatter.5.cloned.1.call-update) | async-done | bytes 262160 | tf_op jit(solution)/shard_map/reduce_scatter | solution.py:58
  238.9 1.7 copy_bitcast_fusion.1
  (27 shorter events, 0.5 us)
Async XLA Ops:
  7.2 56.2 %copy-start = (bf16[64,256]{1,0:T(8,128)(2,1)S(1)}, bf16[64,256]{1,0:T(8,128)(2,1)}, u32[]{:S(2)}) copy-start(bf16[64,256]{1,0:T(8,128)(2,1)} %param.8) | copy-start | bytes 98308
  7.2 45.9 %all-gather.2.cloned.1.call-start = ((), (), s32[]{:S(2)}) async-start(), calls=%async_computation.2 | async-start | bytes 1179648 | tf_op jit(solution)/shard_map/all_gather | solution.py:19
  7.9 81.0 %reduce-scatter.7.cloned.1.call-start = ((), (), s32[]{:S(2)}) async-start(), calls=%async_computation.5 | async-start | bytes 1310720 | tf_op jit(solution)/shard_map/reduce_scatter | solution.py:36
  8.9 4.5 %copy-start.4 = (s32[96]{0:T(128)S(1)}, s32[96]{0:T(128)}, u32[]{:S(2)}) copy-start(s32[96]{0:T(128)} %param.13) | copy-start | bytes 1156
  9.0 4.5 %copy-start.5 = (s32[96,1]{0,1:T(1,128)S(1)}, s32[96,1]{0,1:T(1,128)}, u32[]{:S(2)}) copy-start(s32[96,1]{0,1:T(1,128)} %param.12) | copy-start | bytes 1156
  9.0 4.6 %copy-start.3 = (s32[96]{0:T(128)S(1)}, s32[96]{0:T(128)}, u32[]{:S(2)}) copy-start(s32[96]{0:T(128)} %param.11) | copy-start | bytes 1156
  63.4 25.5 %copy-start.2 = (bf16[64,1024]{1,0:T(8,128)(2,1)S(1)}, bf16[64,1024]{1,0:T(8,128)(2,1)}, u32[]{:S(2)}) copy-start(bf16[64,1024]{1,0:T(8,128)(2,1)} %param.9) | copy-start | bytes 393220
  65.1 102.4 %all-reduce.2.cloned.1.call-start = ((), (), s32[]{:S(2)}) async-start(), calls=%async_computation.4 | async-start | bytes 131072 | tf_op jit(solution)/shard_map/psum | solution.py:63
  98.5 140.4 %reduce-scatter.5.cloned.1.call-start = ((), (), s32[]{:S(2)}) async-start(), calls=%async_computation.3 | async-start | bytes 2359296 | tf_op jit(solution)/shard_map/reduce_scatter | solution.py:58
  115.4 1.3 copy-start.1
Sparse Core Ops, SparseCore 0:
  10.2 42.8 all-gather.1
  65.2 23.6 reduce-scatter.6
  98.7 68.7 all-reduce.1
  171.3 67.5 reduce-scatter.4
where the time goes:
time: 248 us; the launch traced here: 247 us
  waiting for transfers between devices  184 us (74%)
  other arithmetic  20.6 us (8%)
  matrix products  14.9 us (6%)
  between operations  14 us (6%)
  blocking collectives  6.78 us (3%)
  local copies, waits for them, and re-layouts  6.18 us (2%)
    reduce_scatter x1, waiting for transfers between devices, per_device(): lax.psum_scatter(empty.at[target].add(partials, mode='drop'), 'dom', scat...  69.9 us
    psum x1, waiting for transfers between devices, per_device(): weight_grad = lax.psum(weight_terms, 'dom') / math.sqrt(nodes_all)  50.7 us
    all_gather x1, waiting for transfers between devices, per_device(): gathered = lax.all_gather(embed, 'dom', axis=1, tiled=True)  39.4 us
    reduce_scatter x1, waiting for transfers between devices, per_device(): lax.psum_scatter(jnp.einsum('fh,fn->hn', weight, aggregate, preferred_ele...  23.7 us
    scatter-add x1, other arithmetic, per_device(): empty.at[target].add(partials, mode='drop')  10.2 us
    all_gather x1, blocking collectives, per_device(): grad_full = lax.all_gather(grad_pre, 'feat', axis=0, tiled=True)  6.78 us
    dot_general x1, matrix products, per_device(): jnp.einsum('fti,tij->tfj', selected, mask_bf, preferred_element_type=jnp....  5.45 us
    dot_general x1, matrix products, per_device(): jnp.einsum('ftj,tij->fti', fetched, mask_bf, preferred_element_type=jnp.f...  5 us
  transfers between devices with their start and end apart: 4, of which 4 were waited for; matrix products, arithmetic and copies ran while one was open for 10% of the time, Pallas kernels for 0%

commit v1 on v0

v1 whole, which is shorter than its diff:
```python
import functools
import math

import jax
import jax.numpy as jnp
from jax import lax
from jax.experimental import pallas as pl
from jax.experimental.pallas import tpu as pltpu
from jax.sharding import PartitionSpec as P

MESH = pl.DeviceIdType.MESH
VMEM = pl.BlockSpec(memory_space=pltpu.VMEM)
SMEM = pl.BlockSpec(memory_space=pltpu.SMEM)
ANY = pl.BlockSpec(memory_space=pl.ANY)
ONES = 16
CHUNK = 16
VMEM_LIMIT = 56 * 1024 * 1024


def greet(dom_mates, feat_mates):
    barrier = pltpu.get_barrier_semaphore()
    for mate in dom_mates:
        pl.semaphore_signal(barrier, inc=1, device_id={"dom": mate}, device_id_type=MESH)
    for mate in feat_mates:
        pl.semaphore_signal(barrier, inc=1, device_id={"feat": mate}, device_id_type=MESH)
    pl.semaphore_wait(barrier, len(dom_mates) + len(feat_mates))


def send(src, dst, send_sem, recv_sem, **where):
    return pltpu.make_async_remote_copy(
        src_ref=src,
        dst_ref=dst,
        send_sem=send_sem,
        recv_sem=recv_sem,
        device_id=where,
        device_id_type=MESH,
    )


def places(n):
    me = lax.axis_index("dom")
    half = n // 2
    high, low = me // 2, lax.rem(me, 2)
    ahead = [lax.rem(high + k, half) for k in range(half)]
    behind = [lax.rem(high + half - k, half) for k in range(half)]
    return me, low, ahead, behind


def gather_kernel(
    n, f, embed, cot, weight, masks, gath, cot_all, w_all, masks_bf,
    raw, raw_sem, z_send, z_recv, x_send, x_recv, f_send, f_recv,
):
    me, low, ahead, behind = places(n)
    half = n // 2
    feat = lax.axis_index("feat")
    partner = me + 1 - 2 * low
    tiles = masks.shape[0]
    pieces = tiles // CHUNK
    loads = [
        pltpu.make_async_copy(
            masks.at[pl.ds(c * CHUNK, CHUNK)], raw.at[pl.ds(c * CHUNK, CHUNK)], raw_sem.at[c]
        )
        for c in range(pieces)
    ]
    for load in loads:
        load.start()
    feat_mates = [lax.rem(feat + k, f) for k in range(1, f)]
    greet([ahead[k] * 2 + low for k in range(1, half)] + [partner], feat_mates)
    z_copies = [
        send(embed, gath.at[me], z_send.at[k], z_recv.at[k], dom=ahead[k] * 2 + low)
        for k in range(1, half)
    ]
    x_copies = [send(embed, gath.at[me], x_send.at[0], x_recv.at[0], dom=partner)]
    for k in range(1, half):
        slot = gath.at[behind[k] * 2 + low]
        x_copies.append(send(slot, slot, x_send.at[k], x_recv.at[k], dom=partner))
    f_copies = []
    for k in range(1, f):
        f_copies.append(
            send(weight, w_all.at[feat], f_send.at[0, k], f_recv.at[0, k], feat=feat_mates[k - 1])
        )
        f_copies.append(
            send(cot, cot_all.at[feat], f_send.at[1, k], f_recv.at[1, k], feat=feat_mates[k - 1])
        )
    for copy in z_copies + x_copies[:1] + f_copies:
        copy.start()
    gath[me] = embed[...]
    cot_all[feat] = cot[...]
    w_all[feat] = weight[...]
    forwarded = 0
    for c in range(pieces):
        loads[c].wait()

        @pl.loop(c * CHUNK, (c + 1) * CHUNK)
        def _(t):
            masks_bf[t] = raw[t].astype(jnp.float32).astype(jnp.bfloat16)

        if c >= 2 and forwarded < half - 1:
            z_copies[forwarded].wait_recv()
            x_copies[forwarded + 1].start()
            forwarded += 1
    while forwarded < half - 1:
        z_copies[forwarded].wait_recv()
        x_copies[forwarded + 1].start()
        forwarded += 1
    for copy in f_copies + x_copies:
        copy.wait()
    for copy in z_copies:
        copy.wait_send()


def forward_kernel(rows, owner, sub, gath, masks_bf, embed, agg, inv_root, acc):
    tiles, block, _ = masks_bf.shape
    width, local_nodes = embed.shape
    blocks = local_nodes // block
    acc[...] = jnp.zeros_like(acc)
    ones = jnp.ones((ONES, block), jnp.bfloat16)

    def step(t, carry):
        columns = pl.ds(pl.multiple_of(sub[t] * block, block), block)
        taken = jnp.concatenate([gath[owner[t], :, columns], ones], axis=0)
        part = lax.dot_general(
            taken, masks_bf[t], (((1,), (1,)), ((), ())), preferred_element_type=jnp.float32
        )
        acc[rows[t]] += part
        return carry

    lax.fori_loop(0, tiles, step, 0, unroll=8)
    for b in range(blocks):
        columns = slice(b * block, (b + 1) * block)
        root = 1.0 / jnp.sqrt(1.0 + acc[b, width : width + 1, :])
        inv_root[:, columns] = root
        agg[:, columns] = (
            embed[:, columns].astype(jnp.float32) + acc[b, :width, :] * root
        ).astype(jnp.bfloat16)


def dense_kernel(
    f, agg, w_all, weight, cot_all, inv_root, out, grad_agg, scaled, w_terms,
    agg_all, out_all, f_send, f_recv,
):
    feat = lax.axis_index("feat")
    width, local_nodes = agg.shape
    full = f * width
    feat_mates = [lax.rem(feat + k, f) for k in range(1, f)]
    greet([], feat_mates)
    copies = [
        send(agg, agg_all.at[feat], f_send.at[k], f_recv.at[k], feat=feat_mates[k - 1])
        for k in range(1, f)
    ]
    for copy in copies:
        copy.start()
    agg_all[feat] = agg[...]
    whole_w = w_all[...].reshape(full, full)
    for copy in copies:
        copy.wait()
    step = min(256, local_nodes)
    w_terms[...] = jnp.zeros_like(w_terms)

    @pl.loop(0, local_nodes // step)
    def _(c):
        columns = pl.ds(pl.multiple_of(c * step, step), step)
        values = agg_all[:, :, columns].reshape(full, step)
        pre = lax.dot_general(
            whole_w, values, (((0,), (0,)), ((), ())), preferred_element_type=jnp.float32
        )
        gate = jax.nn.sigmoid(pre)
        out_all[:, :, columns] = (pre * gate).astype(jnp.bfloat16).reshape(f, width, step)
        cot = cot_all[:, :, columns].reshape(full, step).astype(jnp.float32)
        grad = (cot * gate * (1.0 + pre * (1.0 - gate))).astype(jnp.bfloat16)
        back = jnp.dot(weight[...], grad, preferred_element_type=jnp.float32)
        grad_agg[:, columns] = back
        scaled[:, columns] = (back * inv_root[:, columns]).astype(jnp.bfloat16)
        w_terms[...] += lax.dot_general(
            agg[:, columns], grad, (((1,), (1,)), ((), ())), preferred_element_type=jnp.float32
        )

    out[...] = out_all[feat]


def backward_kernel(rows, owner, sub, scaled, masks_bf, part, acc):
    tiles, block, _ = masks_bf.shape
    owners = acc.shape[0]

    @pl.loop(0, owners)
    def _(o):
        acc[o] = jnp.zeros_like(acc[o])

    def step(t, carry):
        taken = scaled[:, pl.ds(pl.multiple_of(rows[t] * block, block), block)]
        columns = pl.ds(pl.multiple_of(sub[t] * block, block), block)
        acc[owner[t], :, columns] += jnp.dot(
            taken, masks_bf[t], preferred_element_type=jnp.float32
        )
        return carry

    lax.fori_loop(0, tiles, step, 0, unroll=8)

    @pl.loop(0, owners)
    def _(o):
        part[o] = acc[o].astype(jnp.bfloat16)


def reduce_kernel(
    n, scale, part, grad_agg, w_terms, embed_grad, weight_grad,
    x_buf, z_out, z_buf, w_sum, w_buf, x_send, x_recv, z_send, z_recv, w_send, w_recv,
):
    me, low, ahead, behind = places(n)
    half = n // 2
    partner = me + 1 - 2 * low
    greet([ahead[k] * 2 + low for k in range(1, half)] + [partner], [])
    order = list(range(1, half)) + [0]
    x_copies = {
        k: send(part.at[ahead[k] * 2 + 1 - low], x_buf.at[k], x_send.at[k], x_recv.at[k], dom=partner)
        for k in order
    }
    z_copies = {
        k: send(z_out.at[k], z_buf.at[k], z_send.at[k], z_recv.at[k], dom=ahead[k] * 2 + low)
        for k in range(1, half)
    }
    rounds = n.bit_length() - 1
    w_copies = []
    for b in range(rounds):
        bit = lax.rem(me // (1 << b), 2)
        mate = me + (1 - 2 * bit) * (1 << b)
        src = w_terms if b == 0 else w_sum.at[b - 1]
        w_copies.append(send(src, w_buf.at[b], w_send.at[b], w_recv.at[b], dom=mate))
    w_copies[0].start()
    for k in order:
        x_copies[k].start()

    def w_round(b):
        w_copies[b].wait_recv()
        held = w_terms[...] if b == 0 else w_sum[b - 1]
        total = held + w_buf[b]
        if b == rounds - 1:
            weight_grad[...] = total * scale
        else:
            w_sum[b] = total
            w_copies[b + 1].start()

    done = 0
    for k in order:
        if done < rounds:
            w_round(done)
            done += 1
        x_copies[k].wait_recv()
        total = x_buf[k].astype(jnp.float32) + part[ahead[k] * 2 + low].astype(jnp.float32)
        if k:
            z_out[k] = total.astype(jnp.bfloat16)
            z_copies[k].start()
        else:
            embed_grad[...] = grad_agg[...] + total
    while done < rounds:
        w_round(done)
        done += 1
    for k in range(1, half):
        z_copies[k].wait_recv()
        embed_grad[...] += z_buf[k].astype(jnp.float32)
    for copy in list(x_copies.values()) + list(z_copies.values()) + w_copies:
        copy.wait_send()


def params(collective_id=None):
    if collective_id is None:
        return pltpu.CompilerParams(vmem_limit_bytes=VMEM_LIMIT)
    return pltpu.CompilerParams(
        collective_id=collective_id, has_side_effects=True, vmem_limit_bytes=VMEM_LIMIT
    )


def per_device(embed, weight, cotangent, edge_masks, tile_rows, tile_owner, tile_sub):
    width, local_nodes = embed.shape
    tiles, block, _ = edge_masks.shape
    blocks = local_nodes // block
    n = lax.axis_size("dom")
    f = lax.axis_size("feat")
    full = f * width
    half = n // 2
    rounds = n.bit_length() - 1
    bf, f32 = jnp.bfloat16, jnp.float32
    dma = pltpu.SemaphoreType.DMA
    owner = tile_owner.reshape(tiles)

    gath, cot_all, w_all, masks_bf = pl.pallas_call(
        functools.partial(gather_kernel, n, f),
        out_shape=(
            jax.ShapeDtypeStruct((n, width, local_nodes), bf),
            jax.ShapeDtypeStruct((f, width, local_nodes), bf),
            jax.ShapeDtypeStruct((f, width, full), bf),
            jax.ShapeDtypeStruct((tiles, block, block), bf),
        ),
        in_specs=[VMEM, VMEM, VMEM, ANY],
        out_specs=(VMEM,) * 4,
        scratch_shapes=[
            pltpu.VMEM((tiles, block, block), jnp.int32),
            dma((tiles // CHUNK,)),
            dma((half,)),
            dma((half,)),
            dma((half,)),
            dma((half,)),
            dma((2, f)),
            dma((2, f)),
        ],
        compiler_params=params(0),
        name="gather",
    )(embed, cotangent, weight, edge_masks)

    agg, inv_root = pl.pallas_call(
        forward_kernel,
        out_shape=(
            jax.ShapeDtypeStruct((width, local_nodes), bf),
            jax.ShapeDtypeStruct((1, local_nodes), f32),
        ),
        in_specs=[SMEM] * 3 + [VMEM] * 3,
        out_specs=(VMEM,) * 2,
        scratch_shapes=[pltpu.VMEM((blocks, width + ONES, block), f32)],
        compiler_params=params(),
        name="forward",
    )(tile_rows, owner, tile_sub, gath, masks_bf, embed)

    output, grad_agg, scaled, w_terms = pl.pallas_call(
        functools.partial(dense_kernel, f),
        out_shape=(
            jax.ShapeDtypeStruct((width, local_nodes), bf),
            jax.ShapeDtypeStruct((width, local_nodes), f32),
            jax.ShapeDtypeStruct((width, local_nodes), bf),
            jax.ShapeDtypeStruct((width, full), f32),
        ),
        in_specs=[VMEM] * 5,
        out_specs=(VMEM,) * 4,
        scratch_shapes=[
            pltpu.VMEM((f, width, local_nodes), bf),
            pltpu.VMEM((f, width, local_nodes), bf),
            dma((f,)),
            dma((f,)),
        ],
        compiler_params=params(1),
        name="dense",
    )(agg, w_all, weight, cot_all, inv_root)

    part = pl.pallas_call(
        backward_kernel,
        out_shape=jax.ShapeDtypeStruct((n, width, local_nodes), bf),
        in_specs=[SMEM] * 3 + [VMEM] * 2,
        out_specs=VMEM,
        scratch_shapes=[pltpu.VMEM((n, width, local_nodes), f32)],
        compiler_params=params(),
        name="backward",
    )(tile_rows, owner, tile_sub, scaled, masks_bf)

    embed_grad, weight_grad = pl.pallas_call(
        functools.partial(reduce_kernel, n, 1.0 / math.sqrt(n * local_nodes)),
        out_shape=(
            jax.ShapeDtypeStruct((width, local_nodes), f32),
            jax.ShapeDtypeStruct((width, full), f32),
        ),
        in_specs=[VMEM] * 3,
        out_specs=(VMEM,) * 2,
        scratch_shapes=[
            pltpu.VMEM((half, width, local_nodes), bf),
            pltpu.VMEM((half, width, local_nodes), bf),
            pltpu.VMEM((half, width, local_nodes), bf),
            pltpu.VMEM((rounds, width, full), f32),
            pltpu.VMEM((rounds, width, full), f32),
            dma((half,)),
            dma((half,)),
            dma((half,)),
            dma((half,)),
            dma((rounds,)),
            dma((rounds,)),
        ],
        compiler_params=params(2),
        name="reduce",
    )(part, grad_agg, w_terms)
    return (output, embed_grad, weight_grad)


def solution(mesh):
    in_specs = (
        P("feat", "dom"),
        P("feat", None),
        P("feat", "dom"),
        P("dom", None, None),
        P("dom"),
        P("dom", None),
        P("dom"),
    )
    out_specs = (P("feat", "dom"), P("feat", "dom"), P("feat", None))
    return jax.shard_map(
        per_device, mesh=mesh, in_specs=in_specs, out_specs=out_specs, check_vma=False
    )
```

time: 248 us -> 82.2 us (0.33)
  waiting for transfers between devices: 184 us -> 0 us
  Pallas kernels: 0 us -> 76.5 us
  other arithmetic: 20.6 us -> 0 us
  matrix products: 14.9 us -> 0 us
  between operations: 14 us -> 0.66 us
  blocking collectives: 6.78 us -> 0 us
    reduce_scatter x2 -> x0, waiting for transfers between devices: 93.6 us -> none  [the longest x1 69.9 us: per_device(): lax.psum_scatter(empty.at[target].add(partials, mode='drop'), 'dom', scat...]
    pallas_call x0 -> x5, Pallas kernels: none -> 76.5 us  [the longest x1 27 us: per_device(): pl.pallas_call(functools.partial(reduce_kernel, n, 1.0 / math.sqrt(n * lo...]
    psum x1 -> x0, waiting for transfers between devices: 50.7 us -> none  [per_device(): weight_grad = lax.psum(weight_terms, 'dom') / math.sqrt(nodes_all)]
    all_gather x1 -> x0, waiting for transfers between devices: 39.4 us -> none  [per_device(): gathered = lax.all_gather(embed, 'dom', axis=1, tiled=True)]
    dot_general x7 -> x0, matrix products: 14.9 us -> none  [the longest x1 5.45 us: per_device(): jnp.einsum('fti,tij->tfj', selected, mask_bf, preferred_element_type=jnp....]
    scatter-add x1 -> x0, other arithmetic: 10.2 us -> none  [per_device(): empty.at[target].add(partials, mode='drop')]
    all_gather x1 -> x0, blocking collectives: 6.78 us -> none  [per_device(): grad_full = lax.all_gather(grad_pre, 'feat', axis=0, tiled=True)]
    reduce_sum x1 -> x0, other arithmetic: 4.49 us -> none  [per_device(): counts = jnp.sum(edge_masks, axis=2)]
  transfers between devices with their start and end apart: 4 -> 0, of which waited for: 4 -> 0; matrix products, arithmetic and copies ran while one was open for 10% -> 0% of each run, Pallas kernels for 0% -> 0%
where the time goes in v1:
time: 82.2 us; the launch traced here: 81.9 us
  Pallas kernels  76.5 us (93%)
  local copies, waits for them, and re-layouts  4.71 us (6%)
    pallas_call x1, Pallas kernels, per_device(): pl.pallas_call(functools.partial(reduce_kernel, n, 1.0 / math.sqrt(n * lo...  27 us
    pallas_call x1, Pallas kernels, per_device(): pl.pallas_call(functools.partial(gather_kernel, n, f), out_shape=(jax.Sha...  26.1 us
    pallas_call x1, Pallas kernels, per_device(): pl.pallas_call(functools.partial(dense_kernel, f), out_shape=(jax.ShapeDt...  10.9 us
    pallas_call x1, Pallas kernels, per_device(): pl.pallas_call(forward_kernel, out_shape=(jax.ShapeDtypeStruct((width, lo...  6.67 us
    pallas_call x1, Pallas kernels, per_device(): pl.pallas_call(backward_kernel, out_shape=jax.ShapeDtypeStruct((n, width,...  5.84 us
    unnamed x3, local copies, waits for them, and re-layouts  4.71 us

profile of v1, /device:TPU:0, one launch (start us, length us, event | category | flops | bytes accessed | tf_op | source)
XLA Modules:
  0.0 81.9 jit_solution(4229297937840664681)
XLA Ops:
  0.6 26.1 %gather.1 = (bf16[8,64,1024]{2,1,0:T(8,128)(2,1)}, bf16[4,64,1024]{2,1,0:T(8,128)(2,1)}, bf16[4,64,256]{2,1,0:T(8,128)(2,1)}, bf16[96,128,128]{2,1,0:T(8,128)(2,1)}) custom-call(bf16[64,1024]{1,0:T(8,128)(2,1)} %embed.3, bf16[64,1024]{1,0:T(8,128)(2,1)} %cot.1, bf16[64,256]{1,0:T(8,128)(2,1)} %weight.3, s32[96,128,128]{2,1,0:T(8,128)} %masks.1), custom_call_target="tpu_custom_call" | custom-call | tf_op jit(solution)/shard_map/gather/pallas_call | solution.py:285
  26.7 6.7 %forward.1 = (bf16[64,1024]{1,0:T(8,128)(2,1)}, f32[1,1024]{1,0:T(1,128)}) custom-call(s32[96]{0:T(128)} %rows.3, s32[96]{0:T(128)} %bitcast.1, s32[96]{0:T(128)} %sub.3, bf16[8,64,1024]{2,1,0:T(8,128)(2,1)} %get-tuple-element.15.gath, bf16[96,128,128]{2,1,0:T(8,128)(2,1)} %get-tuple-element.16.masks_bf, bf16[64,1024]{1,0:T(8,128)(2,1)} %embed.3), custom_call_target="tpu_custom_call" | custom-call | tf_op jit(solution)/shard_map/forward/pallas_call | solution.py:309
  33.4 10.9 %dense.1 = (bf16[64,1024]{1,0:T(8,128)(2,1)}, f32[64,1024]{1,0:T(8,128)}, bf16[64,1024]{1,0:T(8,128)(2,1)}, f32[64,256]{1,0:T(8,128)}) custom-call(bf16[64,1024]{1,0:T(8,128)(2,1)} %get-tuple-element.17.agg, bf16[4,64,256]{2,1,0:T(8,128)(2,1)} %get-tuple-element.18.w_all, bf16[64,256]{1,0:T(8,128)(2,1)} %weight.3, ...), custom_call_target="tpu_custom_call" | custom-call | tf_op jit(solution)/shard_map/dense/pallas_call | solution.py:322
  44.3 5.8 %backward.1.part = bf16[8,64,1024]{2,1,0:T(8,128)(2,1)} custom-call(s32[96]{0:T(128)} %rows.3, s32[96]{0:T(128)} %bitcast.2, s32[96]{0:T(128)} %sub.3, bf16[64,1024]{1,0:T(8,128)(2,1)} %get-tuple-element.22.scaled, bf16[96,128,128]{2,1,0:T(8,128)(2,1)} %get-tuple-element.16.masks_bf), custom_call_target="tpu_custom_call" | custom-call | tf_op jit(solution)/shard_map/backward/pallas_call | solution.py:342
  50.1 27.0 %reduce.1 = (f32[64,1024]{1,0:T(8,128)}, f32[64,256]{1,0:T(8,128)}) custom-call(bf16[8,64,1024]{2,1,0:T(8,128)(2,1)} %backward.1.part, f32[64,1024]{1,0:T(8,128)} %get-tuple-element.23.grad_agg, f32[64,256]{1,0:T(8,128)} %get-tuple-element.24.w_terms), custom_call_target="tpu_custom_call" | custom-call | tf_op jit(solution)/shard_map/reduce/pallas_call | solution.py:352
  77.2 1.6 %copy.13 = bf16[64,1024]{1,0:T(8,128)(2,1)} copy(bf16[64,1024]{1,0:T(8,128)(2,1)} %get-tuple-element.30) | data formatting | bytes 262144
  78.7 1.7 %copy.14 = f32[64,1024]{1,0:T(8,128)} copy(f32[64,1024]{1,0:T(8,128)} %get-tuple-element.31) | data formatting | bytes 524288
  80.4 1.5 %copy.15 = f32[64,256]{1,0:T(8,128)} copy(f32[64,256]{1,0:T(8,128)} %get-tuple-element.32) | data formatting | bytes 131072

commit v2 on v1

v2 whole, which is shorter than its diff:
```python
import functools
import math

import jax
import jax.numpy as jnp
from jax import lax
from jax.experimental import pallas as pl
from jax.experimental.pallas import tpu as pltpu
from jax.sharding import PartitionSpec as P

MESH = pl.DeviceIdType.MESH
VMEM = pl.BlockSpec(memory_space=pltpu.VMEM)
SMEM = pl.BlockSpec(memory_space=pltpu.SMEM)
ANY = pl.BlockSpec(memory_space=pl.ANY)
ONES = 16
CHUNK = 16
PIECES = 4
VMEM_LIMIT = 56 * 1024 * 1024


def greet(dom_mates, feat_mates):
    barrier = pltpu.get_barrier_semaphore()
    for mate in dom_mates:
        pl.semaphore_signal(barrier, inc=1, device_id={"dom": mate}, device_id_type=MESH)
    for mate in feat_mates:
        pl.semaphore_signal(barrier, inc=1, device_id={"feat": mate}, device_id_type=MESH)
    pl.semaphore_wait(barrier, len(dom_mates) + len(feat_mates))


def send(src, dst, send_sem, recv_sem, **where):
    return pltpu.make_async_remote_copy(
        src_ref=src,
        dst_ref=dst,
        send_sem=send_sem,
        recv_sem=recv_sem,
        device_id=where,
        device_id_type=MESH,
    )


def places(axis, n):
    me = lax.axis_index(axis)
    half = n // 2
    high, low = me // 2, lax.rem(me, 2)
    ahead = [lax.rem(high + k, half) for k in range(half)]
    behind = [lax.rem(high + half - k, half) for k in range(half)]
    return me, low, me + 1 - 2 * low, ahead, behind


def mates(axis, n):
    _, low, partner, ahead, _ = places(axis, n)
    return [ahead[k] * 2 + low for k in range(1, n // 2)] + [partner]


class Gather:
    def __init__(self, axis, n, src, dst, sems, pieces):
        me, low, partner, ahead, behind = places(axis, n)
        half = n // 2
        rows = src.shape[0] // pieces
        self.first, self.second, self.own = [], [], []
        for p in range(pieces):
            part = pl.ds(p * rows, rows)
            for k in range(1, half):
                self.first.append(
                    send(
                        src.at[part], dst.at[me, part], sems.at[0, k, p], sems.at[1, k, p],
                        **{axis: ahead[k] * 2 + low},
                    )
                )
                slot = dst.at[behind[k] * 2 + low, part]
                self.second.append(
                    send(slot, slot, sems.at[2, k, p], sems.at[3, k, p], **{axis: partner})
                )
            self.own.append(
                send(
                    src.at[part], dst.at[me, part], sems.at[2, 0, p], sems.at[3, 0, p],
                    **{axis: partner},
                )
            )
        self.at = 0

    def start(self):
        per = len(self.first) // len(self.own)
        for p, copy in enumerate(self.own):
            copy.start()
            for other in self.first[p * per : (p + 1) * per]:
                other.start()

    def forward(self, count):
        for _ in range(count):
            if self.at < len(self.first):
                self.first[self.at].wait_recv()
                self.second[self.at].start()
                self.at += 1

    def finish(self):
        self.forward(len(self.first))
        for copy in self.first:
            copy.wait_send()
        for copy in self.own + self.second:
            copy.wait()


def gather_kernel(
    n, f, embed, cot, weight, masks, gath, cot_all, w_all, masks_bf,
    raw, narrow, raw_sem, bf_sem, e_sems, c_sems, w_sems,
):
    tiles = masks.shape[0]
    pieces = tiles // CHUNK
    spans = [pl.ds(c * CHUNK, CHUNK) for c in range(pieces)]
    loads = [
        pltpu.make_async_copy(masks.at[s], raw.at[s], raw_sem.at[c]) for c, s in enumerate(spans)
    ]
    stores = [
        pltpu.make_async_copy(narrow.at[s], masks_bf.at[s], bf_sem.at[c])
        for c, s in enumerate(spans)
    ]
    for load in loads:
        load.start()
    greet(mates("dom", n), mates("feat", f))
    e_gather = Gather("dom", n, embed, gath, e_sems, PIECES)
    c_gather = Gather("feat", f, cot, cot_all, c_sems, PIECES)
    w_gather = Gather("feat", f, weight, w_all, w_sems, 1)
    for gather in (e_gather, w_gather, c_gather):
        gather.start()
    gath[lax.axis_index("dom")] = embed[...]
    cot_all[lax.axis_index("feat")] = cot[...]
    w_all[lax.axis_index("feat")] = weight[...]
    for c in range(pieces):
        loads[c].wait()

        @pl.loop(c * CHUNK, (c + 1) * CHUNK)
        def _(t):
            narrow[t] = raw[t].astype(jnp.float32).astype(jnp.bfloat16)

        stores[c].start()
        if c >= 2:
            e_gather.forward(2)
    w_gather.forward(1)
    e_gather.forward(2)
    c_gather.forward(PIECES)
    for gather in (e_gather, w_gather, c_gather):
        gather.finish()
    for store in stores:
        store.wait()


def forward_kernel(rows, owner, sub, gath, masks_bf, embed, agg, inv_root, acc):
    tiles, block, _ = masks_bf.shape
    width, local_nodes = embed.shape
    blocks = local_nodes // block
    acc[...] = jnp.zeros_like(acc)
    ones = jnp.ones((ONES, block), jnp.bfloat16)

    def step(t, carry):
        columns = pl.ds(pl.multiple_of(sub[t] * block, block), block)
        taken = jnp.concatenate([gath[owner[t], :, columns], ones], axis=0)
        part = lax.dot_general(
            taken, masks_bf[t], (((1,), (1,)), ((), ())), preferred_element_type=jnp.float32
        )
        acc[rows[t]] += part
        return carry

    lax.fori_loop(0, tiles, step, 0, unroll=8)
    for b in range(blocks):
        columns = slice(b * block, (b + 1) * block)
        root = 1.0 / jnp.sqrt(1.0 + acc[b, width : width + 1, :])
        inv_root[:, columns] = root
        agg[:, columns] = (
            embed[:, columns].astype(jnp.float32) + acc[b, :width, :] * root
        ).astype(jnp.bfloat16)


def share_kernel(f, agg, agg_all, sems):
    greet([], mates("feat", f))
    gather = Gather("feat", f, agg, agg_all, sems, PIECES)
    gather.start()
    agg_all[lax.axis_index("feat")] = agg[...]
    gather.finish()


def backward_kernel(
    f, rows, owner, sub, feat, agg, agg_all, w_all, weight, cot_all, inv_root, masks_bf,
    out, grad_agg, w_terms, part, scaled, out_all, acc,
):
    width, local_nodes = agg.shape
    full = f * width
    whole_w = w_all[...].reshape(full, full)
    step = min(256, local_nodes)
    w_terms[...] = jnp.zeros_like(w_terms)

    @pl.loop(0, local_nodes // step)
    def _(c):
        columns = pl.ds(pl.multiple_of(c * step, step), step)
        values = agg_all[:, :, columns].reshape(full, step)
        pre = lax.dot_general(
            whole_w, values, (((0,), (0,)), ((), ())), preferred_element_type=jnp.float32
        )
        gate = jax.nn.sigmoid(pre)
        out_all[:, :, columns] = (pre * gate).astype(jnp.bfloat16).reshape(f, width, step)
        cot = cot_all[:, :, columns].reshape(full, step).astype(jnp.float32)
        grad = (cot * gate * (1.0 + pre * (1.0 - gate))).astype(jnp.bfloat16)
        back = jnp.dot(weight[...], grad, preferred_element_type=jnp.float32)
        grad_agg[:, columns] = back
        scaled[:, columns] = (back * inv_root[:, columns]).astype(jnp.bfloat16)
        w_terms[...] += lax.dot_general(
            agg[:, columns], grad, (((1,), (1,)), ((), ())), preferred_element_type=jnp.float32
        )

    out[...] = out_all[feat[0]]
    tiles, block, _ = masks_bf.shape
    owners = acc.shape[0]

    @pl.loop(0, owners)
    def _(o):
        acc[o] = jnp.zeros_like(acc[o])

    def tile(t, carry):
        taken = scaled[:, pl.ds(pl.multiple_of(rows[t] * block, block), block)]
        columns = pl.ds(pl.multiple_of(sub[t] * block, block), block)
        acc[owner[t], :, columns] += jnp.dot(
            taken, masks_bf[t], preferred_element_type=jnp.float32
        )
        return carry

    lax.fori_loop(0, tiles, tile, 0, unroll=8)

    @pl.loop(0, owners)
    def _(o):
        part[o] = acc[o].astype(jnp.bfloat16)


def reduce_kernel(
    n, part, w_terms, total, w_total,
    x_buf, z_out, z_buf, w_sum, w_buf, sems, w_send, w_recv,
):
    me, low, partner, ahead, behind = places("dom", n)
    half = n // 2
    greet(mates("dom", n), [])
    order = list(range(1, half)) + [0]
    rows = part.shape[1] // PIECES
    spans = [pl.ds(p * rows, rows) for p in range(PIECES)]
    steps = [(p, k) for p in range(PIECES) for k in order]
    x_copies = {
        (p, k): send(
            part.at[ahead[k] * 2 + 1 - low, spans[p]], x_buf.at[k, spans[p]],
            sems.at[0, k, p], sems.at[1, k, p], dom=partner,
        )
        for p, k in steps
    }
    z_copies = {
        (p, k): send(
            z_out.at[k, spans[p]], z_buf.at[k, spans[p]],
            sems.at[2, k, p], sems.at[3, k, p], dom=ahead[k] * 2 + low,
        )
        for p, k in steps
        if k
    }
    rounds = n.bit_length() - 1
    w_copies = []
    for b in range(rounds):
        bit = lax.rem(me // (1 << b), 2)
        mate = me + (1 - 2 * bit) * (1 << b)
        src = w_terms if b == 0 else w_sum.at[b - 1]
        w_copies.append(send(src, w_buf.at[b], w_send.at[b], w_recv.at[b], dom=mate))
    for k in order:
        x_copies[0, k].start()
    w_copies[0].start()
    for p, k in steps[half:]:
        x_copies[p, k].start()

    def w_round(b):
        w_copies[b].wait_recv()
        held = w_terms[...] if b == 0 else w_sum[b - 1]
        summed = held + w_buf[b]
        if b == rounds - 1:
            w_total[...] = summed
        else:
            w_sum[b] = summed
            w_copies[b + 1].start()

    for i, (p, k) in enumerate(steps):
        if i % half == 0 and 0 < i // half <= rounds:
            w_round(i // half - 1)
        x_copies[p, k].wait_recv()
        span = spans[p]
        value = x_buf[k, span].astype(jnp.float32) + part[ahead[k] * 2 + low, span].astype(
            jnp.float32
        )
        if k:
            z_out[k, span] = value.astype(jnp.bfloat16)
            z_copies[p, k].start()
        else:
            total[span] = value
    for b in range(PIECES - 1, rounds):
        w_round(b)
    for p in range(PIECES):
        span = spans[p]
        value = total[span]
        for k in range(1, half):
            z_copies[p, k].wait_recv()
            value += z_buf[k, span].astype(jnp.float32)
        total[span] = value
    for copy in list(x_copies.values()) + list(z_copies.values()) + w_copies:
        copy.wait_send()


def finish_kernel(scale, total, grad_agg, w_total, embed_grad, weight_grad):
    embed_grad[...] = grad_agg[...] + total[...]
    weight_grad[...] = w_total[...] * scale


def params(collective_id=None):
    if collective_id is None:
        return pltpu.CompilerParams(vmem_limit_bytes=VMEM_LIMIT)
    return pltpu.CompilerParams(
        collective_id=collective_id, has_side_effects=True, vmem_limit_bytes=VMEM_LIMIT
    )


def per_device(embed, weight, cotangent, edge_masks, tile_rows, tile_owner, tile_sub):
    width, local_nodes = embed.shape
    tiles, block, _ = edge_masks.shape
    blocks = local_nodes // block
    n = lax.axis_size("dom")
    f = lax.axis_size("feat")
    full = f * width
    half = n // 2
    rounds = n.bit_length() - 1
    bf, f32 = jnp.bfloat16, jnp.float32
    dma = pltpu.SemaphoreType.DMA
    owner = tile_owner.reshape(tiles)

    gath, cot_all, w_all, masks_bf = pl.pallas_call(
        functools.partial(gather_kernel, n, f),
        out_shape=(
            jax.ShapeDtypeStruct((n, width, local_nodes), bf),
            jax.ShapeDtypeStruct((f, width, local_nodes), bf),
            jax.ShapeDtypeStruct((f, width, full), bf),
            jax.ShapeDtypeStruct((tiles, block, block), bf),
        ),
        in_specs=[VMEM, VMEM, VMEM, ANY],
        out_specs=(VMEM, VMEM, VMEM, ANY),
        scratch_shapes=[
            pltpu.VMEM((tiles, block, block), jnp.int32),
            pltpu.VMEM((tiles, block, block), bf),
            dma((tiles // CHUNK,)),
            dma((tiles // CHUNK,)),
            dma((4, half, PIECES)),
            dma((4, f // 2, PIECES)),
            dma((4, f // 2, 1)),
        ],
        compiler_params=params(0),
        name="gather",
    )(embed, cotangent, weight, edge_masks)

    agg, inv_root = pl.pallas_call(
        forward_kernel,
        out_shape=(
            jax.ShapeDtypeStruct((width, local_nodes), bf),
            jax.ShapeDtypeStruct((1, local_nodes), f32),
        ),
        in_specs=[SMEM] * 3 + [VMEM] * 3,
        out_specs=(VMEM,) * 2,
        scratch_shapes=[pltpu.VMEM((blocks, width + ONES, block), f32)],
        compiler_params=params(),
        name="forward",
    )(tile_rows, owner, tile_sub, gath, masks_bf, embed)

    agg_all = pl.pallas_call(
        functools.partial(share_kernel, f),
        out_shape=jax.ShapeDtypeStruct((f, width, local_nodes), bf),
        in_specs=[VMEM],
        out_specs=VMEM,
        scratch_shapes=[dma((4, f // 2, PIECES))],
        compiler_params=params(1),
        name="share",
    )(agg)

    output, grad_agg, w_terms, part = pl.pallas_call(
        functools.partial(backward_kernel, f),
        out_shape=(
            jax.ShapeDtypeStruct((width, local_nodes), bf),
            jax.ShapeDtypeStruct((width, local_nodes), f32),
            jax.ShapeDtypeStruct((width, full), f32),
            jax.ShapeDtypeStruct((n, width, local_nodes), bf),
        ),
        in_specs=[SMEM] * 4 + [VMEM] * 7,
        out_specs=(VMEM,) * 4,
        scratch_shapes=[
            pltpu.VMEM((width, local_nodes), bf),
            pltpu.VMEM((f, width, local_nodes), bf),
            pltpu.VMEM((n, width, local_nodes), f32),
        ],
        compiler_params=params(),
        name="backward",
    )(
        tile_rows, owner, tile_sub, lax.axis_index("feat").reshape(1).astype(jnp.int32),
        agg, agg_all, w_all, weight, cot_all, inv_root, masks_bf,
    )

    total, w_total = pl.pallas_call(
        functools.partial(reduce_kernel, n),
        out_shape=(
            jax.ShapeDtypeStruct((width, local_nodes), f32),
            jax.ShapeDtypeStruct((width, full), f32),
        ),
        in_specs=[VMEM] * 2,
        out_specs=(VMEM,) * 2,
        scratch_shapes=[
            pltpu.VMEM((half, width, local_nodes), bf),
            pltpu.VMEM((half, width, local_nodes), bf),
            pltpu.VMEM((half, width, local_nodes), bf),
            pltpu.VMEM((rounds, width, full), f32),
            pltpu.VMEM((rounds, width, full), f32),
            dma((4, half, PIECES)),
            dma((rounds,)),
            dma((rounds,)),
        ],
        compiler_params=params(2),
        name="reduce",
    )(part, w_terms)

    embed_grad, weight_grad = pl.pallas_call(
        functools.partial(finish_kernel, 1.0 / math.sqrt(n * local_nodes)),
        out_shape=(
            jax.ShapeDtypeStruct((width, local_nodes), f32),
            jax.ShapeDtypeStruct((width, full), f32),
        ),
        in_specs=[VMEM] * 3,
        out_specs=(VMEM,) * 2,
        compiler_params=params(),
        name="finish",
    )(total, grad_agg, w_total)
    return (output, embed_grad, weight_grad)


def solution(mesh):
    in_specs = (
        P("feat", "dom"),
        P("feat", None),
        P("feat", "dom"),
        P("dom", None, None),
        P("dom"),
        P("dom", None),
        P("dom"),
    )
    out_specs = (P("feat", "dom"), P("feat", "dom"), P("feat", None))
    return jax.shard_map(
        per_device, mesh=mesh, in_specs=in_specs, out_specs=out_specs, check_vma=False
    )
```

time: 82.2 us -> 76.5 us (0.931)
  local copies, waits for them, and re-layouts: 4.71 us -> 0 us
  Pallas kernels: 76.5 us -> 75.6 us
    unnamed x3 -> x0, local copies, waits for them, and re-layouts: 4.71 us -> none
    pallas_call x1, Pallas kernels: 26.1 us -> 24.3 us  [per_device(): pl.pallas_call(functools.partial(gather_kernel, n, f), out_shape=(jax.Sha...]
    pallas_call x3 -> x4, Pallas kernels: 43.8 us -> 44.7 us  [the longest x1 25.8 us: per_device(): pl.pallas_call(functools.partial(reduce_kernel, n), out_shape=(jax.ShapeD...]
where the time goes in v2:
time: 76.5 us; the launch traced here: 76.3 us
  Pallas kernels  75.6 us (99%)
    pallas_call x1, Pallas kernels, per_device(): pl.pallas_call(functools.partial(reduce_kernel, n), out_shape=(jax.ShapeD...  25.8 us
    pallas_call x1, Pallas kernels, per_device(): pl.pallas_call(functools.partial(gather_kernel, n, f), out_shape=(jax.Sha...  24.3 us
    pallas_call x1, Pallas kernels, per_device(): pl.pallas_call(functools.partial(share_kernel, f), out_shape=jax.ShapeDty...  8.85 us
    pallas_call x1, Pallas kernels, per_device(): pl.pallas_call(functools.partial(backward_kernel, f), out_shape=(jax.Shap...  8.27 us
    pallas_call x1, Pallas kernels, per_device(): pl.pallas_call(forward_kernel, out_shape=(jax.ShapeDtypeStruct((width, lo...  6.68 us
    pallas_call x1, Pallas kernels, per_device(): pl.pallas_call(functools.partial(finish_kernel, 1.0 / math.sqrt(n * local...  1.78 us

profile of v2, /device:TPU:0, one launch (start us, length us, event | category | flops | bytes accessed | tf_op | source)
XLA Modules:
  0.0 76.3 jit_solution(1019325586039010611)
XLA Ops:
  0.6 24.3 %gather.1 = (bf16[8,64,1024]{2,1,0:T(8,128)(2,1)}, bf16[4,64,1024]{2,1,0:T(8,128)(2,1)}, bf16[4,64,256]{2,1,0:T(8,128)(2,1)}, bf16[96,128,128]{2,1,0:T(8,128)(2,1)}) custom-call(bf16[64,1024]{1,0:T(8,128)(2,1)} %embed.3, bf16[64,1024]{1,0:T(8,128)(2,1)} %cot.1, bf16[64,256]{1,0:T(8,128)(2,1)} %weight.3, s32[96,128,128]{2,1,0:T(8,128)} %masks.1), custom_call_target="tpu_custom_call" | custom-call | tf_op jit(solution)/shard_map/gather/pallas_call | solution.py:334
  24.9 6.7 %forward.1 = (bf16[64,1024]{1,0:T(8,128)(2,1)}, f32[1,1024]{1,0:T(1,128)}) custom-call(s32[96]{0:T(128)} %rows.3, s32[96]{0:T(128)} %bitcast.2, s32[96]{0:T(128)} %sub.3, bf16[8,64,1024]{2,1,0:T(8,128)(2,1)} %get-tuple-element.17.gath, bf16[96,128,128]{2,1,0:T(8,128)(2,1)} %get-tuple-element.18.masks_bf, bf16[64,1024]{1,0:T(8,128)(2,1)} %embed.3), custom_call_target="tpu_custom_call" | custom-call | tf_op jit(solution)/shard_map/forward/pallas_call | solution.py:357
  31.6 8.8 %share.1.agg_all = bf16[4,64,1024]{2,1,0:T(8,128)(2,1)} custom-call(bf16[64,1024]{1,0:T(8,128)(2,1)} %get-tuple-element.19.agg), custom_call_target="tpu_custom_call" | custom-call | tf_op jit(solution)/shard_map/share/pallas_call | solution.py:370
  40.5 8.3 %backward.1 = (bf16[64,1024]{1,0:T(8,128)(2,1)}, f32[64,1024]{1,0:T(8,128)}, f32[64,256]{1,0:T(8,128)}, bf16[8,64,1024]{2,1,0:T(8,128)(2,1)}) custom-call(s32[96]{0:T(128)} %rows.3, s32[96]{0:T(128)} %bitcast.3, s32[96]{0:T(128)} %sub.3, s32[1]{0:T(128)} %bitcast.1.feat, bf16[64,1024]{1,0:T(8,128)(2,1)} %get-tuple-element.19.agg, ...), custom_call_target="tpu_custom_call" | custom-call | tf_op jit(solution)/shard_map/backward/pallas_call | solution.py:380
  48.7 25.8 %reduce.1 = (f32[64,1024]{1,0:T(8,128)}, f32[64,256]{1,0:T(8,128)}) custom-call(bf16[8,64,1024]{2,1,0:T(8,128)(2,1)} %get-tuple-element.24.part, f32[64,256]{1,0:T(8,128)} %get-tuple-element.25.w_terms), custom_call_target="tpu_custom_call" | custom-call | tf_op jit(solution)/shard_map/reduce/pallas_call | solution.py:402
  74.5 1.8 %finish.1 = (f32[64,1024]{1,0:T(8,128)}, f32[64,256]{1,0:T(8,128)}) custom-call(f32[64,1024]{1,0:T(8,128)} %get-tuple-element.26.total, f32[64,1024]{1,0:T(8,128)} %get-tuple-element.27.grad_agg, f32[64,256]{1,0:T(8,128)} %get-tuple-element.28.w_total), custom_call_target="tpu_custom_call" | custom-call | tf_op jit(solution)/shard_map/finish/pallas_call | solution.py:424

commit v3 on v0

v3 whole, which is shorter than its diff:
```python
import functools
import math

import jax
import jax.numpy as jnp
from jax import lax
from jax.experimental import pallas as pl
from jax.experimental.pallas import tpu as pltpu
from jax.sharding import PartitionSpec as P

MESH = pl.DeviceIdType.MESH
VMEM = pl.BlockSpec(memory_space=pltpu.VMEM)
ANY = pl.BlockSpec(memory_space=pl.ANY)
ONES = 16
CHUNK = 16
PIECES = 4
VMEM_LIMIT = 56 * 1024 * 1024


def greet(dom_mates, feat_mates):
    barrier = pltpu.get_barrier_semaphore()
    for mate in dom_mates:
        pl.semaphore_signal(barrier, inc=1, device_id={"dom": mate}, device_id_type=MESH)
    for mate in feat_mates:
        pl.semaphore_signal(barrier, inc=1, device_id={"feat": mate}, device_id_type=MESH)
    pl.semaphore_wait(barrier, len(dom_mates) + len(feat_mates))


def send(src, dst, send_sem, recv_sem, **where):
    return pltpu.make_async_remote_copy(
        src_ref=src,
        dst_ref=dst,
        send_sem=send_sem,
        recv_sem=recv_sem,
        device_id=where,
        device_id_type=MESH,
    )


def places(axis, n):
    me = lax.axis_index(axis)
    half = n // 2
    high, low = me // 2, lax.rem(me, 2)
    ahead = [lax.rem(high + k, half) for k in range(half)]
    behind = [lax.rem(high + half - k, half) for k in range(half)]
    return me, low, me + 1 - 2 * low, ahead, behind


def mates(axis, n):
    _, low, partner, ahead, _ = places(axis, n)
    return [ahead[k] * 2 + low for k in range(1, n // 2)] + [partner]


class Gather:
    def __init__(self, axis, n, src, dst, sems, pieces):
        me, low, partner, ahead, behind = places(axis, n)
        half = n // 2
        rows = src.shape[0] // pieces
        self.pieces = pieces
        self.first, self.second, self.own = [], [], []
        spans = [pl.ds(p * rows, rows) for p in range(pieces)]
        for p, part in enumerate(spans):
            self.own.append(
                send(
                    src.at[part], dst.at[me, part], sems.at[2, 0, p], sems.at[3, 0, p],
                    **{axis: partner},
                )
            )
        for k in range(1, half):
            for p, part in enumerate(spans):
                self.first.append(
                    send(
                        src.at[part], dst.at[me, part], sems.at[0, k, p], sems.at[1, k, p],
                        **{axis: ahead[k] * 2 + low},
                    )
                )
                slot = dst.at[behind[k] * 2 + low, part]
                self.second.append(
                    send(slot, slot, sems.at[2, k, p], sems.at[3, k, p], **{axis: partner})
                )
        self.at = 0

    def start(self):
        for p, copy in enumerate(self.own):
            if self.first:
                self.first[p].start()
            copy.start()
        for copy in self.first[self.pieces :]:
            copy.start()

    def forward(self, count):
        for _ in range(count):
            if self.at < len(self.first):
                self.first[self.at].wait_recv()
                self.second[self.at].start()
                self.at += 1

    def forward_all(self):
        self.forward(len(self.first))

    def arrive(self, k):
        copies = self.own if k == 0 else self.second[(k - 1) * self.pieces : k * self.pieces]
        for copy in copies:
            copy.wait_recv()

    def sent(self):
        for copy in self.first + self.own + self.second:
            copy.wait_send()


def columns_of(b, block):
    return pl.ds(pl.multiple_of(b * block, block), block)


def run_tiles(first, last, step, carry):
    count = last - first
    unroll = 8 if count % 8 == 0 else 1
    return lax.fori_loop(first, last, step, carry, unroll=unroll)


F_TILE, F_OWNER, F_SUB, R_POS, B_TILE, B_ROW, R_LAST, B_LAST = range(8)
R_SAME, B_SAME, R_SOME, B_SOME = range(4)


def fill_orders(n, blocks, tiles, index, table, flags):
    _, low, _, _, _ = places("dom", n)
    high = lax.axis_index("dom") // 2
    half = n // 2
    tp = index.shape[1]
    rows, owner, sub = index[0:1, :], index[1:2, :], index[2:3, :]
    lane = lax.broadcasted_iota(jnp.int32, (tp, tp), 1)
    tile_row = lax.broadcasted_iota(jnp.int32, (1, tp), 1)
    valid = tile_row < tiles
    other = jnp.where(lax.rem(owner, 2) == low, 0, 1)
    owner_high = owner // 2
    arrival = lax.rem(high + half - owner_high, half) * 2 + other
    turn = lax.rem(owner_high + 2 * half - 1 - high, half)
    dest = ((1 - other) * half + turn) * blocks + sub

    def down(row):
        return jnp.broadcast_to(row, (tp, tp)).T

    def ranks(group):
        key = jnp.where(valid, group * tp + tile_row, (1 << 30) + tile_row)
        wide = jnp.broadcast_to(key, (tp, tp))
        before = jnp.where(wide < wide.T, 1, 0)
        group = jnp.broadcast_to(group, (tp, tp))
        alike = jnp.where(group == group.T, before, 0)
        place = jnp.sum(before, axis=1, keepdims=True)
        same = jnp.where(jnp.sum(alike, axis=1, keepdims=True) > 0, 1.0, 0.0)
        return place, same

    def put(ref, slot, rank, column):
        picked = jnp.where(rank == lane, column, jnp.zeros_like(column))
        ref[slot : slot + 1, 0:tp] = jnp.sum(picked, axis=0, keepdims=True)

    def ends(last_slot, some_slot, column, bound):
        lanes = lax.broadcasted_iota(jnp.int32, (tp, bound), 1)
        column = column[:, 0:1]
        upto = jnp.sum(jnp.where(column <= lanes, 1, 0), axis=0, keepdims=True)
        some = jnp.sum(jnp.where(column == lanes, 1, 0), axis=0, keepdims=True)
        table[last_slot : last_slot + 1, 0:bound] = jnp.maximum(upto - 1, 0)
        flags[some_slot : some_slot + 1, 0:bound] = jnp.where(some > 0, 1.0, 0.0)

    table[...] = jnp.zeros_like(table)
    flags[...] = jnp.zeros_like(flags)
    tile_col = down(tile_row)
    row_col = down(jnp.where(valid, rows, 1 << 20))
    dest_col = down(jnp.where(valid, dest, 1 << 20))
    by_arrival, _ = ranks(arrival)
    put(table, F_TILE, by_arrival, tile_col)
    put(table, F_OWNER, by_arrival, down(owner))
    put(table, F_SUB, by_arrival, down(sub))
    by_row, same_row = ranks(rows)
    put(table, R_POS, by_row, by_arrival)
    put(flags, R_SAME, by_row, same_row)
    by_dest, same_dest = ranks(dest)
    put(table, B_TILE, by_dest, tile_col)
    put(table, B_ROW, by_dest, down(rows))
    put(flags, B_SAME, by_dest, same_dest)
    ends(R_LAST, R_SOME, row_col, tp)
    ends(B_LAST, B_SOME, dest_col, table.shape[1])


def layer_kernel(
    n, f, embed, cot, weight, masks, index, out, total, w_total,
    gath, ready, cot_all, w_all, agg, agg_all, out_all, scaled, inv_root, grad_agg, raw, narrow,
    own, table, flags, order, marks, f_parts, f_sums, b_sums, x_buf, z_buf, w_sum, w_buf,
    raw_sem, table_sem, e_sems, c_sems, w_sems, a_sems, r_sems, w_send, w_recv,
):
    me, low, partner, ahead, behind = places("dom", n)
    feat = lax.axis_index("feat")
    half = n // 2
    tiles, block, _ = masks.shape
    width, local_nodes = embed.shape
    blocks = local_nodes // block
    full = f * width
    cap = -(-2 * tiles // n)
    pieces = tiles // CHUNK
    spans = [pl.ds(c * CHUNK, CHUNK) for c in range(pieces)]
    loads = [
        pltpu.make_async_copy(masks.at[s], raw.at[s], raw_sem.at[c]) for c, s in enumerate(spans)
    ]
    for load in loads:
        load.start()
    greet(mates("dom", n), mates("feat", f))
    for b in range(blocks):
        own[b] = embed[:, b * block : (b + 1) * block]
    e_gather = Gather("dom", n, own, gath, e_sems, PIECES)
    c_gather = Gather("feat", f, cot, cot_all, c_sems, PIECES)
    w_gather = Gather("feat", f, weight, w_all, w_sems, 1)
    for gather in (e_gather, w_gather, c_gather):
        gather.start()
    ready[me] = own[...]
    cot_all[feat] = cot[...]
    w_all[feat] = weight[...]
    fill_orders(n, blocks, tiles, index, table, flags)
    to_scalars = [
        pltpu.make_async_copy(table, order, table_sem.at[0]),
        pltpu.make_async_copy(flags, marks, table_sem.at[1]),
    ]
    for copy in to_scalars:
        copy.start()
    for c in range(pieces):
        loads[c].wait()

        @pl.loop(c * CHUNK, (c + 1) * CHUNK)
        def _(t):
            narrow[t] = raw[t].astype(jnp.float32).astype(jnp.bfloat16)

        e_gather.forward(1)
    w_gather.forward_all()
    e_gather.forward_all()
    c_gather.forward_all()
    for copy in to_scalars:
        copy.wait()

    for k in range(1, half):
        ready[behind[k] * 2 + low] = gath[behind[k] * 2 + low]
    ones = jnp.ones((ONES, block), jnp.bfloat16)

    def forward_tile(k, carry):
        taken = ready[order[F_OWNER, k], order[F_SUB, k]]
        f_parts[k] = lax.dot_general(
            jnp.concatenate([taken, ones], axis=0),
            narrow[order[F_TILE, k]],
            (((1,), (1,)), ((), ())),
            preferred_element_type=jnp.float32,
        )
        return carry

    at = 0
    for rank in range(n):
        begin = max(0, tiles - cap * (n - rank))
        if rank % 2:
            if begin > at:
                run_tiles(at, begin, forward_tile, 0)
                at = begin
            e_gather.arrive(rank // 2)
            source = behind[rank // 2] * 2 + 1 - low
            ready[source] = gath[source]
    run_tiles(at, tiles, forward_tile, 0)

    def add_row(k, held):
        held = held * marks[R_SAME, k] + f_parts[order[R_POS, k]]
        f_sums[k] = held
        return held

    run_tiles(0, tiles, add_row, jnp.zeros((width + ONES, block), jnp.float32))

    def segment(sums, last, some, b):
        return sums[order[last, b]] * marks[some, b]

    for b in range(blocks):
        columns = slice(b * block, (b + 1) * block)
        value = segment(f_sums, R_LAST, R_SOME, b)
        root = 1.0 / jnp.sqrt(1.0 + value[width : width + 1, :])
        inv_root[:, columns] = root
        agg[:, columns] = (
            embed[:, columns].astype(jnp.float32) + value[:width, :] * root
        ).astype(jnp.bfloat16)

    a_gather = Gather("feat", f, agg, agg_all, a_sems, PIECES)
    a_gather.start()
    agg_all[feat] = agg[...]
    for k in range(f // 2):
        w_gather.arrive(k)
        c_gather.arrive(k)
    whole_w = w_all[...].reshape(full, full)
    w_total[...] = jnp.zeros_like(w_total)
    a_gather.forward_all()
    for k in range(f // 2):
        a_gather.arrive(k)
    step = 2 * block

    @pl.loop(0, local_nodes // step)
    def _(c):
        columns = columns_of(c, step)
        values = agg_all[:, :, columns].reshape(full, step)
        pre = lax.dot_general(
            whole_w, values, (((0,), (0,)), ((), ())), preferred_element_type=jnp.float32
        )
        gate = jax.nn.sigmoid(pre)
        out_all[:, :, columns] = (pre * gate).astype(jnp.bfloat16).reshape(f, width, step)
        given = cot_all[:, :, columns].reshape(full, step).astype(jnp.float32)
        grad = (given * gate * (1.0 + pre * (1.0 - gate))).astype(jnp.bfloat16)
        back = jnp.dot(weight[...], grad, preferred_element_type=jnp.float32)
        grad_agg[:, columns] = back
        narrowed = (back * inv_root[:, columns]).astype(jnp.bfloat16)
        for b in range(step // block):
            scaled[c * (step // block) + b] = narrowed[:, b * block : (b + 1) * block]
        w_total[...] += lax.dot_general(
            agg[:, columns], grad, (((1,), (1,)), ((), ())), preferred_element_type=jnp.float32
        )

    rounds = n.bit_length() - 1
    w_copies = []
    for b in range(rounds):
        bit = lax.rem(me // (1 << b), 2)
        mate = me + (1 - 2 * bit) * (1 << b)
        w_copies.append(send(w_sum.at[b], w_buf.at[b], w_send.at[b], w_recv.at[b], dom=mate))
    w_sum[0] = w_total[...]
    w_copies[0].start()

    def w_round(b):
        w_copies[b].wait_recv()
        summed = w_sum[b] + w_buf[b]
        if b == rounds - 1:
            w_total[...] = summed * (1.0 / math.sqrt(n * local_nodes))
        else:
            w_sum[b + 1] = summed
            w_copies[b + 1].start()

    turns = list(range(1, half)) + [0]
    group = blocks // PIECES
    parts = [pl.ds(p * group, group) for p in range(PIECES)]
    x_out, z_out = ready.at[pl.ds(0, half)], ready.at[pl.ds(half, half)]
    x_copies = {
        (k, p): send(
            x_out.at[k, part], x_buf.at[k, part], r_sems.at[0, k, p], r_sems.at[1, k, p],
            dom=partner,
        )
        for k in turns
        for p, part in enumerate(parts)
    }
    z_copies = {
        (k, p): send(
            z_out.at[k, part], z_buf.at[k, part], r_sems.at[2, k, p], r_sems.at[3, k, p],
            dom=ahead[k] * 2 + low,
        )
        for k in turns[:-1]
        for p, part in enumerate(parts)
    }

    def backward_tile(k, held):
        held = held * marks[B_SAME, k] + jnp.dot(
            scaled[order[B_ROW, k]],
            narrow[order[B_TILE, k]],
            preferred_element_type=jnp.float32,
        )
        b_sums[k] = held
        return held

    held = jnp.zeros((width, block), jnp.float32)
    at = 0
    for j, k in enumerate(turns):
        upto = min(tiles, cap * (j + 1)) if j < half - 1 else tiles
        held = run_tiles(at, upto, backward_tile, held)
        at = upto
        for b in range(blocks):
            value = segment(b_sums, B_LAST, B_SOME, j * blocks + b)
            x_out[k, b] = value.astype(jnp.bfloat16)
        for p in range(PIECES):
            x_copies[k, p].start()
    for j, k in enumerate(turns):
        for b in range(blocks):
            columns = slice(b * block, (b + 1) * block)
            value = segment(b_sums, B_LAST, B_SOME, (half + j) * blocks + b)
            if k:
                z_out[k, b] = value.astype(jnp.bfloat16)
            else:
                total[:, columns] = grad_agg[:, columns] + value
    for j, k in enumerate(turns):
        for p, part in enumerate(parts):
            x_copies[k, p].wait_recv()
            for b in range(p * group, (p + 1) * group):
                came = x_buf[k, b].astype(jnp.float32)
                if k:
                    z_out[k, b] = (z_out[k, b].astype(jnp.float32) + came).astype(jnp.bfloat16)
                else:
                    total[:, b * block : (b + 1) * block] += came
            if k:
                z_copies[k, p].start()
        if j < rounds:
            w_round(j)
    for b in range(half, rounds):
        w_round(b)
    for k in turns[:-1]:
        for p, part in enumerate(parts):
            z_copies[k, p].wait_recv()
            for b in range(p * group, (p + 1) * group):
                total[:, b * block : (b + 1) * block] += z_buf[k, b].astype(jnp.float32)
    out[...] = out_all[feat]
    for gather in (e_gather, w_gather, c_gather, a_gather):
        gather.sent()
    for copy in list(x_copies.values()) + list(z_copies.values()) + w_copies:
        copy.wait_send()


def finish_kernel(out, total, w_total, output, embed_grad, weight_grad):
    output[...] = out[...]
    embed_grad[...] = total[...]
    weight_grad[...] = w_total[...]


def params(collective_id=None):
    if collective_id is None:
        return pltpu.CompilerParams(vmem_limit_bytes=VMEM_LIMIT)
    return pltpu.CompilerParams(
        collective_id=collective_id, has_side_effects=True, vmem_limit_bytes=VMEM_LIMIT
    )


def per_device(embed, weight, cotangent, edge_masks, tile_rows, tile_owner, tile_sub):
    width, local_nodes = embed.shape
    tiles, block, _ = edge_masks.shape
    blocks = local_nodes // block
    n = lax.axis_size("dom")
    f = lax.axis_size("feat")
    full = f * width
    half = n // 2
    rounds = n.bit_length() - 1
    bf, f32 = jnp.bfloat16, jnp.float32
    dma = pltpu.SemaphoreType.DMA
    lanes = -(-tiles // 128) * 128
    index = jnp.pad(
        jnp.stack([tile_rows, tile_owner.reshape(tiles), tile_sub]), ((0, 0), (0, lanes - tiles))
    )
    table = (8, max(lanes, -(-n * blocks // 128) * 128))
    shard = (width, local_nodes)

    results = (
        jax.ShapeDtypeStruct(shard, bf),
        jax.ShapeDtypeStruct(shard, f32),
        jax.ShapeDtypeStruct((width, full), f32),
    )
    layer = pl.pallas_call(
        functools.partial(layer_kernel, n, f),
        out_shape=results,
        in_specs=[VMEM, VMEM, VMEM, ANY, VMEM],
        out_specs=(VMEM,) * 3,
        scratch_shapes=[
            pltpu.VMEM((n, blocks, width, block), bf),
            pltpu.VMEM((n, blocks, width, block), bf),
            pltpu.VMEM((f, *shard), bf),
            pltpu.VMEM((f, width, full), bf),
            pltpu.VMEM(shard, bf),
            pltpu.VMEM((f, *shard), bf),
            pltpu.VMEM((f, *shard), bf),
            pltpu.VMEM((blocks, width, block), bf),
            pltpu.VMEM((1, local_nodes), f32),
            pltpu.VMEM(shard, f32),
            pltpu.VMEM((tiles, block, block), jnp.int32),
            pltpu.VMEM((tiles, block, block), bf),
            pltpu.VMEM((blocks, width, block), bf),
            pltpu.VMEM(table, jnp.int32),
            pltpu.VMEM(table, f32),
            pltpu.SMEM(table, jnp.int32),
            pltpu.SMEM(table, f32),
            pltpu.VMEM((tiles, width + ONES, block), f32),
            pltpu.VMEM((tiles, width + ONES, block), f32),
            pltpu.VMEM((tiles, width, block), f32),
            pltpu.VMEM((half, blocks, width, block), bf),
            pltpu.VMEM((half, blocks, width, block), bf),
            pltpu.VMEM((rounds, width, full), f32),
            pltpu.VMEM((rounds, width, full), f32),
            dma((tiles // CHUNK,)),
            dma((2,)),
            dma((4, half, PIECES)),
            dma((4, f // 2, PIECES)),
            dma((4, f // 2, 1)),
            dma((4, f // 2, PIECES)),
            dma((4, half, PIECES)),
            dma((rounds,)),
            dma((rounds,)),
        ],
        compiler_params=params(0),
        name="layer",
    )(embed, cotangent, weight, edge_masks, index)
    output, embed_grad, weight_grad = pl.pallas_call(
        finish_kernel,
        out_shape=results,
        in_specs=[VMEM] * 3,
        out_specs=(VMEM,) * 3,
        compiler_params=params(),
        name="finish",
    )(*layer)
    return (output, embed_grad, weight_grad)


def solution(mesh):
    in_specs = (
        P("feat", "dom"),
        P("feat", None),
        P("feat", "dom"),
        P("dom", None, None),
        P("dom"),
        P("dom", None),
        P("dom"),
    )
    out_specs = (P("feat", "dom"), P("feat", "dom"), P("feat", None))
    return jax.shard_map(
        per_device, mesh=mesh, in_specs=in_specs, out_specs=out_specs, check_vma=False
    )
```

time: 248 us -> 58.5 us (0.24)
  waiting for transfers between devices: 184 us -> 0 us
  Pallas kernels: 0 us -> 55.9 us
  other arithmetic: 20.6 us -> 0.7 us
  matrix products: 14.9 us -> 0 us
  between operations: 14 us -> 0.64 us
  blocking collectives: 6.78 us -> 0 us
  local copies, waits for them, and re-layouts: 6.18 us -> 0.58 us
    reduce_scatter x2 -> x0, waiting for transfers between devices: 93.6 us -> none  [the longest x1 69.9 us: per_device(): lax.psum_scatter(empty.at[target].add(partials, mode='drop'), 'dom', scat...]
    pallas_call x0 -> x2, Pallas kernels: none -> 55.9 us  [the longest x1 54.2 us: per_device(): pl.pallas_call(functools.partial(layer_kernel, n, f), out_shape=results,...]
    psum x1 -> x0, waiting for transfers between devices: 50.7 us -> none  [per_device(): weight_grad = lax.psum(weight_terms, 'dom') / math.sqrt(nodes_all)]
    all_gather x1 -> x0, waiting for transfers between devices: 39.4 us -> none  [per_device(): gathered = lax.all_gather(embed, 'dom', axis=1, tiled=True)]
    dot_general x7 -> x0, matrix products: 14.9 us -> none  [the longest x1 5.45 us: per_device(): jnp.einsum('fti,tij->tfj', selected, mask_bf, preferred_element_type=jnp....]
    scatter-add x1 -> x0, other arithmetic: 10.2 us -> none  [per_device(): empty.at[target].add(partials, mode='drop')]
    all_gather x1 -> x0, blocking collectives: 6.78 us -> none  [per_device(): grad_full = lax.all_gather(grad_pre, 'feat', axis=0, tiled=True)]
    reduce_sum x1 -> x0, other arithmetic: 4.49 us -> none  [per_device(): counts = jnp.sum(edge_masks, axis=2)]
  transfers between devices with their start and end apart: 4 -> 0, of which waited for: 4 -> 0; matrix products, arithmetic and copies ran while one was open for 10% -> 0% of each run, Pallas kernels for 0% -> 0%
where the time goes in v3:
time: 58.5 us; the launch traced here: 57.9 us
  Pallas kernels  55.9 us (96%)
  other arithmetic  0.7 us (1%)
  between operations  0.64 us (1%)
    pallas_call x1, Pallas kernels, per_device(): pl.pallas_call(functools.partial(layer_kernel, n, f), out_shape=results,...  54.2 us
    pallas_call x1, Pallas kernels, per_device(): pl.pallas_call(finish_kernel, out_shape=results, in_specs=[VMEM] * 3, out...  1.76 us

profile of v3, /device:TPU:0, one launch (start us, length us, event | category | flops | bytes accessed | tf_op | source)
XLA Modules:
  0.0 57.9 jit_solution(8179818986267319038)
XLA Ops:
  0.6 0.7 %pad_add_fusion = s32[3,96]{1,0:T(4,128)S(1)} fusion(s32[1,96]{1,0:T(1,128)} %bitcast.3, s32[1,96]{1,0:T(1,128)} %bitcast.4, s32[1,96]{1,0:T(1,128)} %bitcast.5), kind=kLoop, calls=%fused_computation | loop fusion | flops 576 | bytes 2304 | tf_op jit(solution)/shard_map/stack | solution.py:437
  1.3 0.6 %pad.4.index = s32[3,128]{1,0:T(4,128)} pad(s32[3,96]{1,0:T(4,128)S(1)} %pad_add_fusion, s32[]{:T(128)} %constant.0.clone.1), padding=0_0x0_32 | pad | bytes 2692 | tf_op jit(solution)/shard_map/jit(_pad)/pad | solution.py:436
  1.9 54.2 %layer.1 = (bf16[64,1024]{1,0:T(8,128)(2,1)}, f32[64,1024]{1,0:T(8,128)}, f32[64,256]{1,0:T(8,128)}) custom-call(bf16[64,1024]{1,0:T(8,128)(2,1)} %embed.1, bf16[64,1024]{1,0:T(8,128)(2,1)} %cot.1, bf16[64,256]{1,0:T(8,128)(2,1)} %weight.1, s32[96,128,128]{2,1,0:T(8,128)} %masks.1, s32[3,128]{1,0:T(4,128)} %pad.4.index), custom_call_target="tpu_custom_call" | custom-call | tf_op jit(solution)/shard_map/layer/pallas_call | solution.py:447
  56.1 1.8 %finish.1 = (bf16[64,1024]{1,0:T(8,128)(2,1)}, f32[64,1024]{1,0:T(8,128)}, f32[64,256]{1,0:T(8,128)}) custom-call(bf16[64,1024]{1,0:T(8,128)(2,1)} %get-tuple-element.6.out, f32[64,1024]{1,0:T(8,128)} %get-tuple-element.7.total, f32[64,256]{1,0:T(8,128)} %get-tuple-element.8.w_total), custom_call_target="tpu_custom_call" | custom-call | tf_op jit(solution)/shard_map/finish/pallas_call | solution.py:490

commit v4 on v3

--- a/solution.py
+++ b/solution.py
@@ -88,6 +88,19 @@
         for copy in self.first[self.pieces :]:
             copy.start()
 
+    def start_piece(self, p):
+        for copy in self.first[p :: self.pieces] + [self.own[p]]:
+            copy.start()
+
+    def forward_piece(self, p):
+        for came, on in zip(self.first[p :: self.pieces], self.second[p :: self.pieces]):
+            came.wait_recv()
+            on.start()
+
+    def arrive_piece(self, p):
+        for copy in [self.own[p]] + self.second[p :: self.pieces]:
+            copy.wait_recv()
+
     def forward(self, count):
         for _ in range(count):
             if self.at < len(self.first):
@@ -108,10 +121,6 @@
             copy.wait_send()
 
 
-def columns_of(b, block):
-    return pl.ds(pl.multiple_of(b * block, block), block)
-
-
 def run_tiles(first, last, step, carry):
     count = last - first
     unroll = 8 if count % 8 == 0 else 1
@@ -122,12 +131,17 @@
 R_SAME, B_SAME, R_SOME, B_SOME = range(4)
 
 
-def fill_orders(n, blocks, tiles, index, table, flags):
+def fill_orders(n, blocks, rows_in, owner_in, sub_in, pad, table, flags):
     _, low, _, _, _ = places("dom", n)
     high = lax.axis_index("dom") // 2
     half = n // 2
-    tp = index.shape[1]
-    rows, owner, sub = index[0:1, :], index[1:2, :], index[2:3, :]
+    tp = pad.shape[1]
+    tiles = owner_in.shape[1]
+    pad[...] = jnp.zeros_like(pad)
+    pad[0:1, 0:tiles] = rows_in[...]
+    pad[1:2, 0:tiles] = owner_in[...]
+    pad[2:3, 0:tiles] = sub_in[...]
+    rows, owner, sub = pad[0:1, :], pad[1:2, :], pad[2:3, :]
     lane = lax.broadcasted_iota(jnp.int32, (tp, tp), 1)
     tile_row = lax.broadcasted_iota(jnp.int32, (1, tp), 1)
     valid = tile_row < tiles
@@ -183,9 +197,9 @@
 
 
 def layer_kernel(
-    n, f, embed, cot, weight, masks, index, out, total, w_total,
+    n, f, embed, cot, weight, masks, rows_in, owner_in, sub_in, out, total, w_total,
     gath, ready, cot_all, w_all, agg, agg_all, out_all, scaled, inv_root, grad_agg, raw, narrow,
-    own, table, flags, order, marks, f_parts, f_sums, b_sums, x_buf, z_buf, w_sum, w_buf,
+    own, pad, table, flags, order, marks, f_parts, f_sums, b_sums, x_buf, z_buf, w_sum, w_buf,
     raw_sem, table_sem, e_sems, c_sems, w_sems, a_sems, r_sems, w_send, w_recv,
 ):
     me, low, partner, ahead, behind = places("dom", n)
@@ -214,7 +228,7 @@
     ready[me] = own[...]
     cot_all[feat] = cot[...]
     w_all[feat] = weight[...]
-    fill_orders(n, blocks, tiles, index, table, flags)
+    fill_orders(n, blocks, rows_in, owner_in, sub_in, pad, table, flags)
     to_scalars = [
         pltpu.make_async_copy(table, order, table_sem.at[0]),
         pltpu.make_async_copy(flags, marks, table_sem.at[1]),
@@ -271,32 +285,29 @@
     def segment(sums, last, some, b):
         return sums[order[last, b]] * marks[some, b]
 
+    a_gather = Gather("feat", f, agg, agg_all, a_sems, PIECES)
+    group = blocks // PIECES
+    step = group * block
     for b in range(blocks):
         columns = slice(b * block, (b + 1) * block)
         value = segment(f_sums, R_LAST, R_SOME, b)
         root = 1.0 / jnp.sqrt(1.0 + value[width : width + 1, :])
         inv_root[:, columns] = root
-        agg[:, columns] = (
-            embed[:, columns].astype(jnp.float32) + value[:width, :] * root
-        ).astype(jnp.bfloat16)
-
-    a_gather = Gather("feat", f, agg, agg_all, a_sems, PIECES)
-    a_gather.start()
+        agg[b] = (embed[:, columns].astype(jnp.float32) + value[:width, :] * root).astype(
+            jnp.bfloat16
+        )
+        if (b + 1) % group == 0:
+            a_gather.start_piece(b // group)
     agg_all[feat] = agg[...]
     for k in range(f // 2):
         w_gather.arrive(k)
         c_gather.arrive(k)
     whole_w = w_all[...].reshape(full, full)
-    w_total[...] = jnp.zeros_like(w_total)
-    a_gather.forward_all()
-    for k in range(f // 2):
-        a_gather.arrive(k)
-    step = 2 * block
-
-    @pl.loop(0, local_nodes // step)
-    def _(c):
-        columns = columns_of(c, step)
-        values = agg_all[:, :, columns].reshape(full, step)
+
+    def dense(p):
+        columns = slice(p * step, (p + 1) * step)
+        held = range(p * group, (p + 1) * group)
+        values = jnp.concatenate([agg_all[:, b].reshape(full, block) for b in held], axis=1)
         pre = lax.dot_general(
             whole_w, values, (((0,), (0,)), ((), ())), preferred_element_type=jnp.float32
         )
@@ -307,11 +318,25 @@
         back = jnp.dot(weight[...], grad, preferred_element_type=jnp.float32)
         grad_agg[:, columns] = back
         narrowed = (back * inv_root[:, columns]).astype(jnp.bfloat16)
-        for b in range(step // block):
-            scaled[c * (step // block) + b] = narrowed[:, b * block : (b + 1) * block]
-        w_total[...] += lax.dot_general(
-            agg[:, columns], grad, (((1,), (1,)), ((), ())), preferred_element_type=jnp.float32
-        )
+        for i, b in enumerate(held):
+            scaled[b] = narrowed[:, i * block : (i + 1) * block]
+        terms = lax.dot_general(
+            jnp.concatenate([agg[b] for b in held], axis=1),
+            grad,
+            (((1,), (1,)), ((), ())),
+            preferred_element_type=jnp.float32,
+        )
+        if p:
+            w_sum[0] += terms
+        else:
+            w_sum[0] = terms
+
+    a_gather.forward_piece(0)
+    for p in range(PIECES):
+        if p + 1 < PIECES:
+            a_gather.forward_piece(p + 1)
+        a_gather.arrive_piece(p)
+        dense(p)
 
     rounds = n.bit_length() - 1
     w_copies = []
@@ -319,7 +344,6 @@
         bit = lax.rem(me // (1 << b), 2)
         mate = me + (1 - 2 * bit) * (1 << b)
         w_copies.append(send(w_sum.at[b], w_buf.at[b], w_send.at[b], w_recv.at[b], dom=mate))
-    w_sum[0] = w_total[...]
     w_copies[0].start()
 
     def w_round(b):
@@ -332,7 +356,6 @@
             w_copies[b + 1].start()
 
     turns = list(range(1, half)) + [0]
-    group = blocks // PIECES
     parts = [pl.ds(p * group, group) for p in range(PIECES)]
     x_out, z_out = ready.at[pl.ds(0, half)], ready.at[pl.ds(half, half)]
     x_copies = {
@@ -380,6 +403,7 @@
                 z_out[k, b] = value.astype(jnp.bfloat16)
             else:
                 total[:, columns] = grad_agg[:, columns] + value
+    out[...] = out_all[feat]
     for j, k in enumerate(turns):
         for p, part in enumerate(parts):
             x_copies[k, p].wait_recv()
@@ -400,7 +424,6 @@
             z_copies[k, p].wait_recv()
             for b in range(p * group, (p + 1) * group):
                 total[:, b * block : (b + 1) * block] += z_buf[k, b].astype(jnp.float32)
-    out[...] = out_all[feat]
     for gather in (e_gather, w_gather, c_gather, a_gather):
         gather.sent()
     for copy in list(x_copies.values()) + list(z_copies.values()) + w_copies:
@@ -433,9 +456,6 @@
     bf, f32 = jnp.bfloat16, jnp.float32
     dma = pltpu.SemaphoreType.DMA
     lanes = -(-tiles // 128) * 128
-    index = jnp.pad(
-        jnp.stack([tile_rows, tile_owner.reshape(tiles), tile_sub]), ((0, 0), (0, lanes - tiles))
-    )
     table = (8, max(lanes, -(-n * blocks // 128) * 128))
     shard = (width, local_nodes)
 
@@ -447,15 +467,15 @@
     layer = pl.pallas_call(
         functools.partial(layer_kernel, n, f),
         out_shape=results,
-        in_specs=[VMEM, VMEM, VMEM, ANY, VMEM],
+        in_specs=[VMEM, VMEM, VMEM, ANY, VMEM, VMEM, VMEM],
         out_specs=(VMEM,) * 3,
         scratch_shapes=[
             pltpu.VMEM((n, blocks, width, block), bf),
             pltpu.VMEM((n, blocks, width, block), bf),
             pltpu.VMEM((f, *shard), bf),
             pltpu.VMEM((f, width, full), bf),
-            pltpu.VMEM(shard, bf),
-            pltpu.VMEM((f, *shard), bf),
+            pltpu.VMEM((blocks, width, block), bf),
+            pltpu.VMEM((f, blocks, width, block), bf),
             pltpu.VMEM((f, *shard), bf),
             pltpu.VMEM((blocks, width, block), bf),
             pltpu.VMEM((1, local_nodes), f32),
@@ -463,6 +483,7 @@
             pltpu.VMEM((tiles, block, block), jnp.int32),
             pltpu.VMEM((tiles, block, block), bf),
             pltpu.VMEM((blocks, width, block), bf),
+            pltpu.VMEM((8, lanes), jnp.int32),
             pltpu.VMEM(table, jnp.int32),
             pltpu.VMEM(table, f32),
             pltpu.SMEM(table, jnp.int32),
@@ -486,7 +507,10 @@
         ],
         compiler_params=params(0),
         name="layer",
-    )(embed, cotangent, weight, edge_masks, index)
+    )(
+        embed, cotangent, weight, edge_masks,
+        tile_rows.reshape(1, tiles), tile_owner.reshape(1, tiles), tile_sub.reshape(1, tiles),
+    )
     output, embed_grad, weight_grad = pl.pallas_call(
         finish_kernel,
         out_shape=results,

time: 58.5 us -> 56.2 us (0.961)
  other arithmetic: 0.7 us -> 0 us
    another operation x1 -> x0, other arithmetic: 0.7 us -> none  [per_device(): jnp.stack([tile_rows, tile_owner.reshape(tiles), tile_sub])]
where the time goes in v4:
time: 56.2 us; the launch traced here: 56 us
  Pallas kernels  55.4 us (99%)
  between operations  0.64 us (1%)
    pallas_call x1, Pallas kernels, per_device(): pl.pallas_call(functools.partial(layer_kernel, n, f), out_shape=results,...  53.6 us
    pallas_call x1, Pallas kernels, per_device(): pl.pallas_call(finish_kernel, out_shape=results, in_specs=[VMEM] * 3, out...  1.76 us

profile of v4, /device:TPU:0, one launch (start us, length us, event | category | flops | bytes accessed | tf_op | source)
XLA Modules:
  0.0 56.0 jit_solution(10477622276594319469)
XLA Ops:
  0.6 53.6 %layer.1 = (bf16[64,1024]{1,0:T(8,128)(2,1)}, f32[64,1024]{1,0:T(8,128)}, f32[64,256]{1,0:T(8,128)}) custom-call(bf16[64,1024]{1,0:T(8,128)(2,1)} %embed.1, bf16[64,1024]{1,0:T(8,128)(2,1)} %cot.1, bf16[64,256]{1,0:T(8,128)(2,1)} %weight.1, s32[96,128,128]{2,1,0:T(8,128)} %masks.1, s32[1,96]{1,0:T(1,128)} %bitcast.3, s32[1,96]{1,0:T(1,128)} %bitcast.4, ...), custom_call_target="tpu_custom_call" | custom-call | tf_op jit(solution)/shard_map/layer/pallas_call | solution.py:467
  54.3 1.8 %finish.1 = (bf16[64,1024]{1,0:T(8,128)(2,1)}, f32[64,1024]{1,0:T(8,128)}, f32[64,256]{1,0:T(8,128)}) custom-call(bf16[64,1024]{1,0:T(8,128)(2,1)} %get-tuple-element.6.out, f32[64,1024]{1,0:T(8,128)} %get-tuple-element.7.total, f32[64,256]{1,0:T(8,128)} %get-tuple-element.8.w_total), custom_call_target="tpu_custom_call" | custom-call | tf_op jit(solution)/shard_map/finish/pallas_call | solution.py:514

commit v5 on v4

--- a/solution.py
+++ b/solution.py
@@ -127,11 +127,24 @@
     return lax.fori_loop(first, last, step, carry, unroll=unroll)
 
 
-F_TILE, F_OWNER, F_SUB, R_POS, B_TILE, B_ROW, R_LAST, B_LAST = range(8)
+F_TILE, F_OWNER, F_SUB, B_TILE, B_ROW, R_LAST, B_LAST = range(7)
 R_SAME, B_SAME, R_SOME, B_SOME = range(4)
 
 
-def fill_orders(n, blocks, rows_in, owner_in, sub_in, pad, table, flags):
+def forward_cuts(n, tiles, cap):
+    cuts, waits = [], []
+    for rank in range(1, n, 2):
+        begin = max(0, tiles - cap * (n - rank))
+        if begin > (cuts[-1] if cuts else 0):
+            cuts.append(begin)
+            waits.append([])
+        if cuts:
+            waits[-1].append(rank // 2)
+    first = [k for k in range(n // 2) if all(k not in some for some in waits)]
+    return [0] + cuts, [first] + waits
+
+
+def fill_orders(n, blocks, cuts, rows_in, owner_in, sub_in, pad, table, flags):
     _, low, _, _, _ = places("dom", n)
     high = lax.axis_index("dom") // 2
     half = n // 2
@@ -179,27 +192,29 @@
     table[...] = jnp.zeros_like(table)
     flags[...] = jnp.zeros_like(flags)
     tile_col = down(tile_row)
-    row_col = down(jnp.where(valid, rows, 1 << 20))
     dest_col = down(jnp.where(valid, dest, 1 << 20))
-    by_arrival, _ = ranks(arrival)
-    put(table, F_TILE, by_arrival, tile_col)
-    put(table, F_OWNER, by_arrival, down(owner))
-    put(table, F_SUB, by_arrival, down(sub))
-    by_row, same_row = ranks(rows)
-    put(table, R_POS, by_row, by_arrival)
+    place, _ = ranks(arrival)
+    group = jnp.zeros_like(place)
+    for cut in cuts[1:]:
+        group += jnp.where(place >= cut, 1, 0)
+    by_group = jnp.broadcast_to(group, (tp, tp)).T[0:1, :] * blocks + rows
+    by_row, same_row = ranks(by_group)
+    put(table, F_TILE, by_row, tile_col)
+    put(table, F_OWNER, by_row, down(owner))
+    put(table, F_SUB, by_row, down(sub))
     put(flags, R_SAME, by_row, same_row)
     by_dest, same_dest = ranks(dest)
     put(table, B_TILE, by_dest, tile_col)
     put(table, B_ROW, by_dest, down(rows))
     put(flags, B_SAME, by_dest, same_dest)
-    ends(R_LAST, R_SOME, row_col, tp)
+    ends(R_LAST, R_SOME, down(jnp.where(valid, by_group, 1 << 20)), table.shape[1])
     ends(B_LAST, B_SOME, dest_col, table.shape[1])
 
 
 def layer_kernel(
     n, f, embed, cot, weight, masks, rows_in, owner_in, sub_in, out, total, w_total,
     gath, ready, cot_all, w_all, agg, agg_all, out_all, scaled, inv_root, grad_agg, raw, narrow,
-    own, pad, table, flags, order, marks, f_parts, f_sums, b_sums, x_buf, z_buf, w_sum, w_buf,
+    own, pad, table, flags, order, marks, f_sums, b_sums, x_buf, z_buf, w_sum, w_buf,
     raw_sem, table_sem, e_sems, c_sems, w_sems, a_sems, r_sems, w_send, w_recv,
 ):
     me, low, partner, ahead, behind = places("dom", n)
@@ -228,7 +243,8 @@
     ready[me] = own[...]
     cot_all[feat] = cot[...]
     w_all[feat] = weight[...]
-    fill_orders(n, blocks, rows_in, owner_in, sub_in, pad, table, flags)
+    cuts, waits = forward_cuts(n, tiles, cap)
+    fill_orders(n, blocks, cuts, rows_in, owner_in, sub_in, pad, table, flags)
     to_scalars = [
         pltpu.make_async_copy(table, order, table_sem.at[0]),
         pltpu.make_async_copy(flags, marks, table_sem.at[1]),
@@ -253,34 +269,24 @@
         ready[behind[k] * 2 + low] = gath[behind[k] * 2 + low]
     ones = jnp.ones((ONES, block), jnp.bfloat16)
 
-    def forward_tile(k, carry):
+    def forward_tile(k, held):
         taken = ready[order[F_OWNER, k], order[F_SUB, k]]
-        f_parts[k] = lax.dot_general(
+        held = held * marks[R_SAME, k] + lax.dot_general(
             jnp.concatenate([taken, ones], axis=0),
             narrow[order[F_TILE, k]],
             (((1,), (1,)), ((), ())),
             preferred_element_type=jnp.float32,
         )
-        return carry
-
-    at = 0
-    for rank in range(n):
-        begin = max(0, tiles - cap * (n - rank))
-        if rank % 2:
-            if begin > at:
-                run_tiles(at, begin, forward_tile, 0)
-                at = begin
-            e_gather.arrive(rank // 2)
-            source = behind[rank // 2] * 2 + 1 - low
-            ready[source] = gath[source]
-    run_tiles(at, tiles, forward_tile, 0)
-
-    def add_row(k, held):
-        held = held * marks[R_SAME, k] + f_parts[order[R_POS, k]]
         f_sums[k] = held
         return held
 
-    run_tiles(0, tiles, add_row, jnp.zeros((width + ONES, block), jnp.float32))
+    held = jnp.zeros((width + ONES, block), jnp.float32)
+    for begin, end, arriving in zip(cuts, cuts[1:] + [tiles], waits):
+        for k in arriving:
+            e_gather.arrive(k)
+            source = behind[k] * 2 + 1 - low
+            ready[source] = gath[source]
+        held = run_tiles(begin, end, forward_tile, held)
 
     def segment(sums, last, some, b):
         return sums[order[last, b]] * marks[some, b]
@@ -291,6 +297,8 @@
     for b in range(blocks):
         columns = slice(b * block, (b + 1) * block)
         value = segment(f_sums, R_LAST, R_SOME, b)
+        for g in range(1, len(cuts)):
+            value += segment(f_sums, R_LAST, R_SOME, g * blocks + b)
         root = 1.0 / jnp.sqrt(1.0 + value[width : width + 1, :])
         inv_root[:, columns] = root
         agg[b] = (embed[:, columns].astype(jnp.float32) + value[:width, :] * root).astype(
@@ -489,7 +497,6 @@
             pltpu.SMEM(table, jnp.int32),
             pltpu.SMEM(table, f32),
             pltpu.VMEM((tiles, width + ONES, block), f32),
-            pltpu.VMEM((tiles, width + ONES, block), f32),
             pltpu.VMEM((tiles, width, block), f32),
             pltpu.VMEM((half, blocks, width, block), bf),
             pltpu.VMEM((half, blocks, width, block), bf),

time: 56.2 us -> 55.8 us (level)
  no operation moved by 1% of the time
where the time goes in v5:
time: 55.8 us; the launch traced here: 55.7 us
  Pallas kernels  55.1 us (99%)
  between operations  0.64 us (1%)
    pallas_call x1, Pallas kernels, per_device(): pl.pallas_call(functools.partial(layer_kernel, n, f), out_shape=results,...  53.3 us
    pallas_call x1, Pallas kernels, per_device(): pl.pallas_call(finish_kernel, out_shape=results, in_specs=[VMEM] * 3, out...  1.76 us

profile of v5, /device:TPU:0, one launch (start us, length us, event | category | flops | bytes accessed | tf_op | source)
XLA Modules:
  0.0 55.7 jit_solution(12530425096334294732)
XLA Ops:
  0.6 53.3 %layer.1 = (bf16[64,1024]{1,0:T(8,128)(2,1)}, f32[64,1024]{1,0:T(8,128)}, f32[64,256]{1,0:T(8,128)}) custom-call(bf16[64,1024]{1,0:T(8,128)(2,1)} %embed.1, bf16[64,1024]{1,0:T(8,128)(2,1)} %cot.1, bf16[64,256]{1,0:T(8,128)(2,1)} %weight.1, s32[96,128,128]{2,1,0:T(8,128)} %masks.1, s32[1,96]{1,0:T(1,128)} %bitcast.3, s32[1,96]{1,0:T(1,128)} %bitcast.4, ...), custom_call_target="tpu_custom_call" | custom-call | tf_op jit(solution)/shard_map/layer/pallas_call | solution.py:475
  53.9 1.8 %finish.1 = (bf16[64,1024]{1,0:T(8,128)(2,1)}, f32[64,1024]{1,0:T(8,128)}, f32[64,256]{1,0:T(8,128)}) custom-call(bf16[64,1024]{1,0:T(8,128)(2,1)} %get-tuple-element.6.out, f32[64,1024]{1,0:T(8,128)} %get-tuple-element.7.total, f32[64,256]{1,0:T(8,128)} %get-tuple-element.8.w_total), custom_call_target="tpu_custom_call" | custom-call | tf_op jit(solution)/shard_map/finish/pallas_call | solution.py:521

commit v6 on v5

--- a/solution.py
+++ b/solution.py
@@ -352,7 +352,6 @@
         bit = lax.rem(me // (1 << b), 2)
         mate = me + (1 - 2 * bit) * (1 << b)
         w_copies.append(send(w_sum.at[b], w_buf.at[b], w_send.at[b], w_recv.at[b], dom=mate))
-    w_copies[0].start()
 
     def w_round(b):
         w_copies[b].wait_recv()
@@ -403,6 +402,8 @@
             x_out[k, b] = value.astype(jnp.bfloat16)
         for p in range(PIECES):
             x_copies[k, p].start()
+        if j == min(1, half - 1):
+            w_copies[0].start()
     for j, k in enumerate(turns):
         for b in range(blocks):
             columns = slice(b * block, (b + 1) * block)

time: 55.8 us -> 57.2 us (1.025)
  Pallas kernels: 55.1 us -> 56.4 us
    pallas_call x1, Pallas kernels: 53.3 us -> 54.7 us  [per_device(): pl.pallas_call(functools.partial(layer_kernel, n, f), out_shape=results,...]
where the time goes in v6:
time: 57.2 us; the launch traced here: 57.1 us
  Pallas kernels  56.4 us (99%)
  between operations  0.64 us (1%)
    pallas_call x1, Pallas kernels, per_device(): pl.pallas_call(functools.partial(layer_kernel, n, f), out_shape=results,...  54.7 us
    pallas_call x1, Pallas kernels, per_device(): pl.pallas_call(finish_kernel, out_shape=results, in_specs=[VMEM] * 3, out...  1.76 us

profile of v6, /device:TPU:0, one launch (start us, length us, event | category | flops | bytes accessed | tf_op | source)
XLA Modules:
  0.0 57.1 jit_solution(17342936732124843127)
XLA Ops:
  0.6 54.7 %layer.1 = (bf16[64,1024]{1,0:T(8,128)(2,1)}, f32[64,1024]{1,0:T(8,128)}, f32[64,256]{1,0:T(8,128)}) custom-call(bf16[64,1024]{1,0:T(8,128)(2,1)} %embed.1, bf16[64,1024]{1,0:T(8,128)(2,1)} %cot.1, bf16[64,256]{1,0:T(8,128)(2,1)} %weight.1, s32[96,128,128]{2,1,0:T(8,128)} %masks.1, s32[1,96]{1,0:T(1,128)} %bitcast.3, s32[1,96]{1,0:T(1,128)} %bitcast.4, ...), custom_call_target="tpu_custom_call" | custom-call | tf_op jit(solution)/shard_map/layer/pallas_call | solution.py:476
  55.3 1.8 %finish.1 = (bf16[64,1024]{1,0:T(8,128)(2,1)}, f32[64,1024]{1,0:T(8,128)}, f32[64,256]{1,0:T(8,128)}) custom-call(bf16[64,1024]{1,0:T(8,128)(2,1)} %get-tuple-element.6.out, f32[64,1024]{1,0:T(8,128)} %get-tuple-element.7.total, f32[64,256]{1,0:T(8,128)} %get-tuple-element.8.w_total), custom_call_target="tpu_custom_call" | custom-call | tf_op jit(solution)/shard_map/finish/pallas_call | solution.py:522
